TPU v7x, 1024 devices: a whole 8x8x8 slice. The times are simulated.
1024 devices in a mesh: hid: 64 (over x, y), wid: 16 (over z, core).
Axes of the slice: x: 8, y: 8, z: 8, core: 2. Of those that a mesh axis runs over, the one named last changes fastest.
Arguments:
- tokens: bfloat16 [256, 16384], P('hid', 'wid'), may hold values from -6 to 6
- gate_weight: bfloat16 [16384, 26624], P('wid', 'hid'), may hold values from -0.046875 to 0.046875
- up_weight: bfloat16 [16384, 26624], P('wid', 'hid'), may hold values from -0.046875 to 0.046875
- down_weight: bfloat16 [26624, 16384], P('hid', 'wid'), may hold values from -0.0390625 to 0.0390625
Outputs:
- stream: bfloat16 [256, 16384], P('hid', 'wid')
All inputs are finite; a program needn't handle non-finite values.
Results may differ from a plain program's by a relative error of at most 0.035.
Values may be sent and summed in bfloat16 or wider, within the bound.
No kernel may reach another device: no remote copies, remote signals or barrier semaphores. Data moves between devices by JAX's collectives and lax.ppermute only.
A program may use at most 32 MiB of HBM per device.

v0:
```python
import jax
import jax.numpy as jnp
from jax import lax
from jax.sharding import PartitionSpec as P

STEPS = 2


def activate(partial_value):
    totals = lax.psum(partial_value.astype(jnp.bfloat16), "wid").astype(jnp.float32)
    return (jax.nn.silu(totals[:, 0]) * totals[:, 1]).astype(jnp.bfloat16)


def per_device(tokens, gate_weight, up_weight, down_weight):
    stream = tokens
    for repeat in range(STEPS):
        shard_rows = lax.all_gather(stream, "hid", axis=0, tiled=True)
        gate_part = jnp.dot(shard_rows, gate_weight, preferred_element_type=jnp.float32)
        up_part = jnp.dot(shard_rows, up_weight, preferred_element_type=jnp.float32)
        partial_value = jnp.stack([gate_part, up_part], axis=1)
        hidden = activate(partial_value)
        branch = lax.psum_scatter(
            jnp.dot(hidden, down_weight, preferred_element_type=jnp.float32),
            "hid",
            scatter_dimension=0,
            tiled=True,
        )
        stream = (stream.astype(jnp.float32) + branch).astype(jnp.bfloat16)
    return stream


def solution(mesh):
    in_specs = (P("hid", "wid"), P("wid", "hid"), P("wid", "hid"), P("hid", "wid"))
    out_specs = P("hid", "wid")
    return jax.shard_map(
        per_device, mesh=mesh, in_specs=in_specs, out_specs=out_specs, check_vma=False
    )
```

profile of v0, /device:TPU:1, one launch (start us, length us, event | category | flops | bytes accessed | tf_op | source)
XLA Modules:
  0.0 712.4 jit_solution(7133321861039560410)
XLA Ops:
  6.5 0.0 copy-start
  6.5 0.0 copy-start.1
  6.5 0.0 all-reduce.7.cloned.1.call-start
  6.5 40.4 %all-gather = bf16[64,4,1024]{2,1,0:T(4,128)(2,1)S(1)} all-gather(bf16[1,4,1024]{2,1,0:T(4,128)(2,1)} %bitcast.46), channel_id=1, replica_groups=mesh['hid'=64,'wid'=16] {'hid'}, dimensions={0}, use_global_device_ids=true | all-gather | bytes 532480 | tf_op jit(solution)/shard_map/all_gather | solution.py:17
  47.0 0.1 reshape.1
  47.1 0.0 copy-done.1
  47.1 0.0 copy-start.2
  47.1 0.4 fusion.1
  47.6 0.7 copy-done.2
  48.3 0.4 fusion
  48.7 0.8 pad_maximum_fusion
  49.5 0.0 all-reduce.7.cloned.1.call-update
  49.5 0.0 all-reduce.11.cloned.1.call-start
  49.6 138.6 %all-reduce.7.cloned.1.call-done = bf16[256,2,416]{0,2,1:T(8,128)(2,1)} async-done(((bf16[256,2,416]{0,2,1:T(8,128)(2,1)}), bf16[256,2,416]{0,2,1:T(8,128)(2,1)}) %all-reduce.7.cloned.1.call-update) | async-done | bytes 426000 | tf_op jit(solution)/shard_map/psum | solution.py:10
  188.2 1.1 convert_element_type.27
  189.3 0.0 copy-done
  189.3 1.5 fusion.8
  190.8 0.0 all-reduce.11.cloned.1.call-update
  190.8 0.0 all-reduce.9.cloned.1.call-start
  190.9 0.0 copy-start.3
  190.9 1.3 dynamic-slice
  192.8 164.5 %all-reduce.11.cloned.1.call-done = f32[256,1024]{1,0:T(8,128)} async-done(((f32[256,1024]{1,0:T(8,128)}), f32[256,1024]{1,0:T(8,128)}) %all-reduce.11.cloned.1.call-update) | async-done | bytes 1048592
  357.3 0.0 copy-done.3
  357.3 0.8 fusion.18
  358.1 39.9 %all-gather.1 = bf16[64,4,1024]{2,1,0:T(4,128)(2,1)} all-gather(bf16[1,4,1024]{2,1,0:T(4,128)(2,1)S(1)} %fusion.18), channel_id=1, replica_groups=mesh['hid'=64,'wid'=16] {'hid'}, dimensions={0}, use_global_device_ids=true | all-gather | bytes 532480 | tf_op jit(solution)/shard_map/all_gather | solution.py:17
  398.0 1.2 reshape.3
  399.1 0.4 fusion.3
  399.6 0.4 fusion.2
  400.0 0.8 pad_maximum_fusion.1
  400.8 0.0 all-reduce.9.cloned.1.call-update
  400.8 0.0 all-reduce.13.cloned.1.call-start
  400.8 134.5 %all-reduce.9.cloned.1.call-done = bf16[256,2,416]{0,2,1:T(8,128)(2,1)} async-done(((bf16[256,2,416]{0,2,1:T(8,128)(2,1)}), bf16[256,2,416]{0,2,1:T(8,128)(2,1)}) %all-reduce.9.cloned.1.call-update) | async-done | bytes 426000 | tf_op jit(solution)/shard_map/psum | solution.py:10
  535.4 1.1 convert_element_type.31
  536.5 1.5 fusion.10
  538.0 0.0 all-reduce.13.cloned.1.call-update
  538.0 166.4 %all-reduce.13.cloned.1.call-done = f32[256,1024]{1,0:T(8,128)} async-done(((f32[256,1024]{1,0:T(8,128)}), f32[256,1024]{1,0:T(8,128)}) %all-reduce.13.cloned.1.call-update) | async-done | bytes 1048592
  704.4 1.4 fusion.14
Async XLA Ops:
  6.5 182.7 %copy-start = (bf16[416,1024]{1,0:T(8,128)(2,1)S(1)}, bf16[416,1024]{1,0:T(8,128)(2,1)}, u32[]{:S(2)}) copy-start(bf16[416,1024]{1,0:T(8,128)(2,1)} %param.7) | copy-start | bytes 2555908
  6.5 40.6 %copy-start.1 = (bf16[1024,416]{0,1:T(8,128)(2,1)S(1)}, bf16[1024,416]{0,1:T(8,128)(2,1)}, u32[]{:S(2)}) copy-start(bf16[1024,416]{0,1:T(8,128)(2,1)} %param.6) | copy-start | bytes 2555908
  6.5 181.6 %all-reduce.7.cloned.1.call-start = ((), (), s32[]{:S(2)}) async-start(), calls=%async_computation | async-start | bytes 851968 | tf_op jit(solution)/shard_map/psum | solution.py:10
  47.1 1.2 copy-start.2
  49.5 307.8 %all-reduce.11.cloned.1.call-start = ((), (), s32[]{:S(2)}) async-start(), calls=%async_computation.2 | async-start | bytes 2097152
  190.8 344.6 %all-reduce.9.cloned.1.call-start = ((), (), s32[]{:S(2)}) async-start(), calls=%async_computation.1 | async-start | bytes 851968 | tf_op jit(solution)/shard_map/psum | solution.py:10
  190.9 166.5 %copy-start.3 = (bf16[4,1024]{1,0:T(4,128)(2,1)S(1)}, bf16[4,1024]{1,0:T(4,128)(2,1)}, u32[]{:S(2)}) copy-start(bf16[4,1024]{1,0:T(4,128)(2,1)} %param.4) | copy-start | bytes 24580
  400.8 303.6 %all-reduce.13.cloned.1.call-start = ((), (), s32[]{:S(2)}) async-start(), calls=%async_computation.3 | async-start | bytes 2097152
Sparse Core Ops, SparseCore 0:
  49.7 138.4 all-reduce.6
  191.7 165.5 all-reduce.10
  400.9 134.4 all-reduce.8
  538.8 165.6 all-reduce.12
where the time goes:
time: 716 us; the launch traced here: 712 us
  waiting for transfers between devices  604 us (84%)
  blocking collectives  80.3 us (11%)
  between operations  13.9 us (2%)
    unnamed x6, waiting for transfers between devices  331 us
    psum x2, waiting for transfers between devices, activate(): lax.psum(partial_value.astype(jnp.bfloat16), 'wid').astype(jnp.float32)  273 us
    all_gather x2, blocking collectives, per_device(): shard_rows = lax.all_gather(stream, 'hid', axis=0, tiled=True)  80.3 us
  transfers between devices with their start and end apart: 4, of which 4 were waited for; matrix products, arithmetic and copies ran while one was open for 0% of the time, Pallas kernels for 0%

commit v1 on v0

v1 whole, which is shorter than its diff:
```python
import jax
import jax.numpy as jnp
from jax import lax
from jax.sharding import PartitionSpec as P

STEPS = 2


def per_device(tokens, gate_weight, up_weight, down_weight):
    n_hid, n_wid = lax.axis_size("hid"), lax.axis_size("wid")
    own, span = tokens.shape
    rows = n_hid * own
    units = gate_weight.shape[1]
    stream = tokens
    for repeat in range(STEPS):
        copies = jnp.broadcast_to(stream[None], (n_hid, own, span))
        shard_rows = lax.all_to_all(copies, "hid", 0, 0, tiled=True).reshape(rows, span)
        gate_part = jnp.dot(shard_rows, gate_weight, preferred_element_type=jnp.float32)
        up_part = jnp.dot(shard_rows, up_weight, preferred_element_type=jnp.float32)
        partial_value = jnp.concatenate(
            [gate_part.astype(jnp.bfloat16), up_part.astype(jnp.bfloat16)], axis=1
        )
        parts = lax.all_to_all(
            partial_value.reshape(n_wid, rows // n_wid, 2 * units), "wid", 0, 0, tiled=True
        )
        totals = jnp.sum(parts.astype(jnp.float32), axis=0)
        own_hidden = (jax.nn.silu(totals[:, :units]) * totals[:, units:]).astype(jnp.bfloat16)
        hidden = lax.all_gather(own_hidden, "wid", axis=0, tiled=True)
        down_part = jnp.dot(hidden, down_weight, preferred_element_type=jnp.float32)
        parts = lax.all_to_all(
            down_part.astype(jnp.bfloat16).reshape(n_hid, own, span), "hid", 0, 0, tiled=True
        )
        branch = jnp.sum(parts.astype(jnp.float32), axis=0)
        stream = (stream.astype(jnp.float32) + branch).astype(jnp.bfloat16)
    return stream


def solution(mesh):
    in_specs = (P("hid", "wid"), P("wid", "hid"), P("wid", "hid"), P("hid", "wid"))
    out_specs = P("hid", "wid")
    return jax.shard_map(
        per_device, mesh=mesh, in_specs=in_specs, out_specs=out_specs, check_vma=False
    )
```

time: 716 us -> 201 us (0.28)
  waiting for transfers between devices: 604 us -> 0 us
  blocking collectives: 80.3 us -> 190 us
  between operations: 13.9 us -> 0.12 us
    unnamed x6 -> x0, waiting for transfers between devices: 331 us -> none
    psum x2 -> x0, waiting for transfers between devices: 273 us -> none  [activate(): lax.psum(partial_value.astype(jnp.bfloat16), 'wid').astype(jnp.float32)]
    all_to_all x0 -> x6, blocking collectives: none -> 159 us  [the longest x2 62.6 us: per_device(): lax.all_to_all(partial_value.reshape(n_wid, rows // n_wid, 2 * units), 'w...]
    all_gather x2, blocking collectives: 80.3 us -> 30.3 us  [per_device(): hidden = lax.all_gather(own_hidden, 'wid', axis=0, tiled=True)]
  transfers between devices with their start and end apart: 4 -> 0, of which waited for: 4 -> 0; matrix products, arithmetic and copies ran while one was open for 0% -> 0% of each run, Pallas kernels for 0% -> 0%
where the time goes in v1:
time: 201 us; the launch traced here: 199 us
  blocking collectives  190 us (95%)
  local copies, waits for them, and re-layouts  5.19 us (3%)
  matrix products  2.57 us (1%)
    all_to_all x2, blocking collectives, per_device(): lax.all_to_all(partial_value.reshape(n_wid, rows // n_wid, 2 * units), 'w...  62.6 us
    all_to_all x2, blocking collectives, per_device(): lax.all_to_all(copies, 'hid', 0, 0, tiled=True).reshape(rows, span)  51.9 us
    all_to_all x2, blocking collectives, per_device(): lax.all_to_all(down_part.astype(jnp.bfloat16).reshape(n_hid, own, span),...  44.7 us
    all_gather x2, blocking collectives, per_device(): hidden = lax.all_gather(own_hidden, 'wid', axis=0, tiled=True)  30.3 us

profile of v1, /device:TPU:1, one launch (start us, length us, event | category | flops | bytes accessed | tf_op | source)
XLA Modules:
  0.0 198.9 jit_solution(11561994525740111701)
XLA Ops:
  0.0 0.0 copy-start
  0.0 0.9 broadcast_in_dim.4
  0.9 0.0 copy-start.1
  0.9 28.5 %all_to_all.30 = bf16[64,4,1024]{2,1,0:T(4,128)(2,1)S(1)} all-to-all(bf16[64,4,1024]{2,1,0:T(4,128)(2,1)S(1)} %broadcast_in_dim.4), channel_id=1, replica_groups=mesh['hid'=64,'wid'=16] {'hid'}, dimensions={0} | all-to-all | bytes 1048576 | tf_op jit(solution)/shard_map/all_to_all | solution.py:17
  29.5 0.1 reshape.20
  29.6 0.0 copy-done.1
  29.6 0.0 copy-start.2
  29.6 0.4 convolution_convert_fusion.4
  30.0 0.7 copy-done.2
  30.8 0.4 convolution_convert_fusion.5
  31.2 0.2 copy.5
  31.5 38.1 %all_to_all.31 = bf16[16,16,832]{2,1,0:T(8,128)(2,1)S(1)} all-to-all(bf16[16,16,832]{2,1,0:T(8,128)(2,1)S(1)} %bitcast.14), channel_id=1, replica_groups=mesh['hid'=64,'wid'=16] {'wid'}, dimensions={0} | all-to-all | bytes 851968 | tf_op jit(solution)/shard_map/all_to_all | solution.py:23
  69.6 0.1 convert_reduce_fusion.3
  69.7 0.1 fusion.1
  69.8 15.2 %all_gather.6 = bf16[256,416]{1,0:T(8,128)(2,1)S(1)} all-gather(bf16[16,416]{1,0:T(8,128)(2,1)S(1)} %fusion.1), channel_id=1, replica_groups=mesh['hid'=64,'wid'=16] {'wid'}, dimensions={0}, use_global_device_ids=true | all-gather | bytes 226304 | tf_op jit(solution)/shard_map/all_gather | solution.py:28
  84.9 0.0 copy-done
  84.9 0.4 convolution_convert_fusion.1
  85.4 1.0 reshape.22
  86.4 22.4 %all_to_all.32 = bf16[64,4,1024]{2,1,0:T(4,128)(2,1)S(1)} all-to-all(bf16[64,4,1024]{2,1,0:T(4,128)(2,1)} %reshape.22), channel_id=1, replica_groups=mesh['hid'=64,'wid'=16] {'hid'}, dimensions={0} | all-to-all | bytes 1048576 | tf_op jit(solution)/shard_map/all_to_all | solution.py:30
  108.7 0.0 copy-start.3
  108.7 0.2 convert_reduce_fusion.1
  109.0 0.5 copy-done.3
  109.4 0.1 broadcast_in_dim.5
  109.6 23.4 %all_to_all.33 = bf16[64,4,1024]{2,1,0:T(4,128)(2,1)} all-to-all(bf16[64,4,1024]{2,1,0:T(4,128)(2,1)S(1)} %broadcast_in_dim.5), channel_id=1, replica_groups=mesh['hid'=64,'wid'=16] {'hid'}, dimensions={0} | all-to-all | bytes 1048576 | tf_op jit(solution)/shard_map/all_to_all | solution.py:17
  132.9 1.2 reshape.23
  134.1 0.4 convolution_convert_fusion.2
  134.5 0.4 convolution_convert_fusion.3
  135.0 0.2 copy.6
  135.3 24.5 %all_to_all.34 = bf16[16,16,832]{2,1,0:T(8,128)(2,1)S(1)} all-to-all(bf16[16,16,832]{2,1,0:T(8,128)(2,1)S(1)} %bitcast.15), channel_id=1, replica_groups=mesh['hid'=64,'wid'=16] {'wid'}, dimensions={0} | all-to-all | bytes 851968 | tf_op jit(solution)/shard_map/all_to_all | solution.py:23
  159.7 0.1 convert_reduce_fusion.2
  159.8 0.1 fusion
  159.9 15.2 %all_gather.7 = bf16[256,416]{1,0:T(8,128)(2,1)S(1)} all-gather(bf16[16,416]{1,0:T(8,128)(2,1)S(1)} %fusion), channel_id=1, replica_groups=mesh['hid'=64,'wid'=16] {'wid'}, dimensions={0}, use_global_device_ids=true | all-gather | bytes 226304 | tf_op jit(solution)/shard_map/all_gather | solution.py:28
  175.0 0.4 convolution_convert_fusion
  175.5 0.2 reshape.25
  175.7 22.3 %all_to_all.35 = bf16[64,4,1024]{2,1,0:T(4,128)(2,1)S(1)} all-to-all(bf16[64,4,1024]{2,1,0:T(4,128)(2,1)S(1)} %reshape.25), channel_id=1, replica_groups=mesh['hid'=64,'wid'=16] {'hid'}, dimensions={0} | all-to-all | bytes 1048576 | tf_op jit(solution)/shard_map/all_to_all | solution.py:30
  198.0 0.2 convert_reduce_fusion
  198.2 0.6 add_convert_fusion
  (3 shorter events, 0.1 us)
Async XLA Ops:
  0.0 84.9 %copy-start = (bf16[416,1024]{1,0:T(8,128)(2,1)S(1)}, bf16[416,1024]{1,0:T(8,128)(2,1)}, u32[]{:S(2)}) copy-start(bf16[416,1024]{1,0:T(8,128)(2,1)} %param.7) | copy-start | bytes 2555908
  0.9 28.7 %copy-start.1 = (bf16[1024,416]{0,1:T(8,128)(2,1)S(1)}, bf16[1024,416]{0,1:T(8,128)(2,1)}, u32[]{:S(2)}) copy-start(bf16[1024,416]{0,1:T(8,128)(2,1)} %param.6) | copy-start | bytes 2555908
  29.6 1.2 copy-start.2
  108.7 0.7 copy-start.3

commit v2 on v1

v2 whole, which is shorter than its diff:
```python
import jax
import jax.numpy as jnp
from jax import lax
from jax.sharding import Mesh, PartitionSpec as P

STEPS = 2
CORES = 2


def product(rows, weight):
    return lax.dot_general(
        rows, weight, (((1,), (1,)), ((), ())), preferred_element_type=jnp.float32
    )


def exchange(parts, axes):
    return lax.all_to_all(parts, axes, 0, 0, tiled=True)


def per_device(tokens, gate_weight, up_weight, down_weight):
    n_hid, n_z = lax.axis_size("hid"), lax.axis_size("z")
    own, span = tokens.shape
    units = gate_weight.shape[1]
    half = own // CORES
    rows = n_hid * half
    core, hid = lax.axis_index("core"), lax.axis_index("hid")
    first = core == 0

    weights = jnp.concatenate([gate_weight.T, up_weight.T, down_weight], axis=0)
    others = lax.ppermute(weights, "core", [(0, 1), (1, 0)])

    copies = jnp.broadcast_to(tokens.reshape(1, CORES, half, span), (n_hid, CORES, half, span))
    gathered = exchange(copies.reshape(n_hid * CORES, half, span), ("hid", "core"))
    gathered = gathered.reshape(n_hid, CORES, half, span)
    low, high = gathered[:, 0], gathered[:, 1]
    gathered = jnp.concatenate(
        [jnp.where(first, low, high), jnp.where(first, high, low)], axis=-1
    )
    stream = lax.dynamic_index_in_dim(gathered, hid, 0, keepdims=False)

    for repeat in range(STEPS):
        if repeat > 0:
            gathered = exchange(
                jnp.broadcast_to(stream[None], (n_hid, half, CORES * span)), "hid"
            )
        shard_rows = gathered.reshape(rows, CORES * span)
        partial_value = product(shard_rows[:, :span], weights[: 2 * units])
        partial_value += product(shard_rows[:, span:], others[: 2 * units])
        parts = exchange(
            partial_value.astype(jnp.bfloat16).reshape(n_z, rows // n_z, 2 * units), "z"
        )
        totals = jnp.sum(parts.astype(jnp.float32), axis=0)
        own_hidden = (jax.nn.silu(totals[:, :units]) * totals[:, units:]).astype(jnp.bfloat16)
        hidden = exchange(
            jnp.broadcast_to(own_hidden[None], (n_z, rows // n_z, units)), "z"
        ).reshape(rows, units)
        here = jnp.dot(hidden, weights[2 * units :], preferred_element_type=jnp.float32)
        there = jnp.dot(hidden, others[2 * units :], preferred_element_type=jnp.float32)
        if repeat < STEPS - 1:
            down_part = jnp.concatenate(
                [here.astype(jnp.bfloat16), there.astype(jnp.bfloat16)], axis=1
            )
            parts = exchange(down_part.reshape(n_hid, half, CORES * span), "hid")
            branch = jnp.sum(parts.astype(jnp.float32), axis=0)
            stream = (stream.astype(jnp.float32) + branch).astype(jnp.bfloat16)

    owner = (jnp.arange(n_hid) == hid)[:, None, None]
    here = here.reshape(n_hid, half, span) + jnp.where(owner, stream[None, :, :span], 0)
    there = there.reshape(n_hid, half, span) + jnp.where(owner, stream[None, :, span:], 0)
    here, there = here.astype(jnp.bfloat16), there.astype(jnp.bfloat16)
    down_part = jnp.stack(
        [jnp.where(first, here, there), jnp.where(first, there, here)], axis=1
    )
    parts = exchange(down_part.reshape(n_hid * CORES, half, span), ("hid", "core"))
    total = jnp.sum(parts.reshape(n_hid, own, span).astype(jnp.float32), axis=0)
    return total.astype(jnp.bfloat16)


def solution(mesh):
    n_hid, n_wid = mesh.devices.shape
    fine = Mesh(mesh.devices.reshape(n_hid, n_wid // CORES, CORES), ("hid", "z", "core"))
    wid = ("z", "core")
    in_specs = (P("hid", wid), P(wid, "hid"), P(wid, "hid"), P("hid", wid))
    out_specs = P("hid", wid)
    return jax.shard_map(
        per_device, mesh=fine, in_specs=in_specs, out_specs=out_specs, check_vma=False
    )
```

time: 201 us -> 198 us (0.985)
  blocking collectives: 190 us -> 63.8 us
  waiting for transfers between devices: 0 us -> 66.2 us
  starting transfers between devices: 0 us -> 43.5 us
  matrix products: 2.57 us -> 10 us
  other arithmetic: 1.46 us -> 6.15 us
    all_to_all x6 -> x3, blocking collectives: 159 us -> 63.8 us  [exchange(): return lax.all_to_all(parts, axes, 0, 0, tiled=True)]
    all_to_all x0 -> x5, waiting for transfers between devices: none -> 66.2 us  [exchange(): return lax.all_to_all(parts, axes, 0, 0, tiled=True)]
    all_gather x2 -> x0, blocking collectives: 30.3 us -> none  [per_device(): hidden = lax.all_gather(own_hidden, 'wid', axis=0, tiled=True)]
    all_to_all x0 -> x5, starting transfers between devices: none -> 27.3 us  [exchange(): return lax.all_to_all(parts, axes, 0, 0, tiled=True)]
    ppermute x0 -> x1, starting transfers between devices: none -> 16.2 us  [per_device(): others = lax.ppermute(weights, 'core', [(0, 1), (1, 0)])]
    dot_general x6 -> x8, matrix products: 2.57 us -> 10 us  [the longest x4 6.45 us: product(): lax.dot_general(rows, weight, (((1,), (1,)), ((), ())), preferred_element...]
    concatenate x2, other arithmetic: 0.06 us -> 3.45 us  [the longest x1 3.41 us: per_device(): weights = jnp.concatenate([gate_weight.T, up_weight.T, down_weight], axis=0)]
  transfers between devices with their start and end apart: 0 -> 6, of which waited for: 0 -> 5; matrix products, arithmetic and copies ran while one was open for 0% -> 2% of each run, Pallas kernels for 0% -> 0%
where the time goes in v2:
time: 198 us; the launch traced here: 197 us
  waiting for transfers between devices  66.2 us (33%)
  blocking collectives  63.8 us (32%)
  starting transfers between devices  43.5 us (22%)
  matrix products  10 us (5%)
  local copies, waits for them, and re-layouts  7.05 us (4%)
  other arithmetic  6.15 us (3%)
    all_to_all x5, waiting for transfers between devices, exchange(): return lax.all_to_all(parts, axes, 0, 0, tiled=True)  66.2 us
    all_to_all x3, blocking collectives, exchange(): return lax.all_to_all(parts, axes, 0, 0, tiled=True)  63.8 us
    all_to_all x5, starting transfers between devices, exchange(): return lax.all_to_all(parts, axes, 0, 0, tiled=True)  27.3 us
    ppermute x1, starting transfers between devices, per_device(): others = lax.ppermute(weights, 'core', [(0, 1), (1, 0)])  16.2 us
    dot_general x4, matrix products, product(): lax.dot_general(rows, weight, (((1,), (1,)), ((), ())), preferred_element...  6.45 us
  transfers between devices with their start and end apart: 6, of which 5 were waited for; matrix products, arithmetic and copies ran while one was open for 2% of the time, Pallas kernels for 0%

profile of v2, /device:TPU:1, one launch (start us, length us, event | category | flops | bytes accessed | tf_op | source)
XLA Modules:
  0.0 197.0 jit_solution(1335140195172914155)
XLA Ops:
  0.0 3.4 %pad_maximum_fusion = bf16[1248,1024]{1,0:T(8,128)(2,1)} fusion(bf16[416,1024]{1,0:T(8,128)(2,1)} %param.7, bf16[416,1024]{1,0:T(8,128)(2,1)} %bitcast.63, bf16[416,1024]{1,0:T(8,128)(2,1)} %bitcast.66), kind=kLoop, calls=%fused_computation | loop fusion | flops 7667712 | bytes 5111808 | tf_op jit(solution)/shard_map/concatenate | solution.py:29
  3.4 16.2 %collective-permute-start = (bf16[1248,1024]{1,0:T(8,128)(2,1)}, bf16[1248,1024]{1,0:T(8,128)(2,1)}, u32[]{:S(2)}, u32[]{:S(2)}) collective-permute-start(bf16[1248,1024]{1,0:T(8,128)(2,1)} %pad_maximum_fusion), channel_id=1, source_target_pairs={{0,1},{1,0},{2,3},{3,2},{4,5},{5,4},{6,7},{7,6},{8,9},{9,8},{10,11... | collective-permute-start | bytes 7667720 | tf_op jit(solution)/shard_map/ppermute | solution.py:30
  19.6 1.1 broadcast_in_dim.60
  20.7 5.3 %all-to-all-start = ((bf16[128,2,1024]{2,1,0:T(2,128)(2,1)}), bf16[128,2,1024]{2,1,0:T(2,128)(2,1)S(1)}, u32[]{:S(2)}, u32[]{:S(2)}) async-start(bf16[128,2,1024]{2,1,0:T(2,128)(2,1)} %bitcast), calls=%async_computation | async-start | bytes 1048576 | tf_op jit(solution)/shard_map/all_to_all | solution.py:17
  26.0 19.4 %all-to-all-done = bf16[128,2,1024]{2,1,0:T(2,128)(2,1)S(1)} async-done(((bf16[128,2,1024]{2,1,0:T(2,128)(2,1)}), bf16[128,2,1024]{2,1,0:T(2,128)(2,1)S(1)}, u32[]{:S(2)}, u32[]{:S(2)}) %all-to-all-start) | async-done | bytes 524320 | tf_op jit(solution)/shard_map/all_to_all | solution.py:17
  45.5 0.3 broadcast_select_fusion
  45.8 0.1 select_n.54
  45.9 0.3 bitcast_select_fusion
  46.1 0.1 select_n.55
  46.3 0.6 fusion.19
  46.9 0.0 copy-start
  46.9 0.0 collective-permute-done
  46.9 2.1 %fusion.15 = bf16[128,832]{0,1:T(8,128)(2,1)S(1)} fusion(f32[128,832]{0,1:T(8,128)S(1)} %fusion.19, bf16[128,1024]{1,0:T(8,128)(2,1)S(1)} %select_n.55, bf16[1248,1024]{1,0:T(8,128)(2,1)} %collective-permute-done), kind=kOutput, calls=%fused_computation.15 | convolution fusion | flops 218316800 | bytes 2605056 | tf_op jit(solution)/shard_map/dot_general | solution.py:11
  49.1 0.2 copy.9
  49.2 21.2 %all_to_all.40 = bf16[8,16,832]{2,1,0:T(8,128)(2,1)S(1)} all-to-all(bf16[8,16,832]{2,1,0:T(8,128)(2,1)S(1)} %bitcast.62), channel_id=1, replica_groups=mesh['hid'=64,'z'=8,'core'=2] {'z'}, dimensions={0} | all-to-all | bytes 425984 | tf_op jit(solution)/shard_map/all_to_all | solution.py:17
  70.5 0.1 fusion.29
  70.6 10.4 %all_to_all.41 = bf16[8,16,416]{2,1,0:T(8,128)(2,1)S(1)} all-to-all(bf16[8,16,416]{2,1,0:T(8,128)(2,1)S(1)} %broadcast_in_dim.61), channel_id=1, replica_groups=mesh['hid'=64,'z'=8,'core'=2] {'z'}, dimensions={0} | all-to-all | bytes 212992 | tf_op jit(solution)/shard_map/all_to_all | solution.py:17
  81.0 0.0 copy-done
  81.0 0.3 convolution_convert_fusion.1
  81.3 1.5 convolution_convert_fusion
  82.8 1.1 reshape.66
  84.0 7.6 %all-to-all-start.3 = ((bf16[64,2,2048]{2,1,0:T(2,128)(2,1)}), bf16[64,2,2048]{2,1,0:T(2,128)(2,1)S(1)}, u32[]{:S(2)}, u32[]{:S(2)}) async-start(bf16[64,2,2048]{2,1,0:T(2,128)(2,1)} %reshape.66), calls=%async_computation.3 | async-start | bytes 1048576 | tf_op jit(solution)/shard_map/all_to_all | solution.py:17
  91.6 0.3 fusion.48
  91.9 0.3 fusion.49
  92.2 15.0 %all-to-all-done.3 = bf16[64,2,2048]{2,1,0:T(2,128)(2,1)S(1)} async-done(((bf16[64,2,2048]{2,1,0:T(2,128)(2,1)}), bf16[64,2,2048]{2,1,0:T(2,128)(2,1)S(1)}, u32[]{:S(2)}, u32[]{:S(2)}) %all-to-all-start.3) | async-done | bytes 524320 | tf_op jit(solution)/shard_map/all_to_all | solution.py:17
  107.2 0.4 convert_reduce_fusion
  107.6 0.0 copy-start.3
  107.6 1.1 broadcast_in_dim.63
  108.7 7.5 %all-to-all-start.4 = ((bf16[64,2,2048]{2,1,0:T(2,128)(2,1)}), bf16[64,2,2048]{2,1,0:T(2,128)(2,1)S(1)}, u32[]{:S(2)}, u32[]{:S(2)}) async-start(bf16[64,2,2048]{2,1,0:T(2,128)(2,1)} %broadcast_in_dim.63), calls=%async_computation.4 | async-start | bytes 1048576 | tf_op jit(solution)/shard_map/all_to_all | solution.py:17
  116.2 15.3 %all-to-all-done.4 = bf16[64,2,2048]{2,1,0:T(2,128)(2,1)S(1)} async-done(((bf16[64,2,2048]{2,1,0:T(2,128)(2,1)}), bf16[64,2,2048]{2,1,0:T(2,128)(2,1)S(1)}, u32[]{:S(2)}, u32[]{:S(2)}) %all-to-all-start.4) | async-done | bytes 524320 | tf_op jit(solution)/shard_map/all_to_all | solution.py:17
  131.5 1.0 reshape.67
  132.5 1.6 fusion.18
  134.2 2.1 %fusion.12 = bf16[128,832]{0,1:T(8,128)(2,1)S(1)} fusion(f32[128,832]{0,1:T(8,128)S(1)} %fusion.18, bf16[1248,1024]{1,0:T(8,128)(2,1)} %collective-permute-done, bf16[128,2048]{1,0:T(8,128)(2,1)S(1)} %copy-done.4), kind=kOutput, calls=%fused_computation.14 | convolution fusion | flops 218316800 | bytes 2605056 | tf_op jit(solution)/shard_map/dot_general | solution.py:11
  136.2 0.8 copy.10
  137.1 3.4 %all-to-all-start.5 = ((bf16[8,16,832]{2,1,0:T(8,128)(2,1)}), bf16[8,16,832]{2,1,0:T(8,128)(2,1)S(1)}, u32[]{:S(2)}, u32[]{:S(2)}) async-start(bf16[8,16,832]{2,1,0:T(8,128)(2,1)} %bitcast.13), calls=%async_computation.5 | async-start | bytes 458752 | tf_op jit(solution)/shard_map/all_to_all | solution.py:17
  140.5 8.9 %all-to-all-done.5 = bf16[8,16,832]{2,1,0:T(8,128)(2,1)S(1)} async-done(((bf16[8,16,832]{2,1,0:T(8,128)(2,1)}), bf16[8,16,832]{2,1,0:T(8,128)(2,1)S(1)}, u32[]{:S(2)}, u32[]{:S(2)}) %all-to-all-start.5) | async-done | bytes 213024 | tf_op jit(solution)/shard_map/all_to_all | solution.py:17
  149.4 0.1 fusion.28
  149.5 0.7 broadcast_in_dim.64
  150.2 3.5 %all-to-all-start.6 = ((bf16[8,16,416]{2,1,0:T(8,128)(2,1)}), bf16[8,16,416]{2,1,0:T(8,128)(2,1)S(1)}, u32[]{:S(2)}, u32[]{:S(2)}) async-start(bf16[8,16,416]{2,1,0:T(8,128)(2,1)} %broadcast_in_dim.64), calls=%async_computation.6 | async-start | bytes 262144 | tf_op jit(solution)/shard_map/all_to_all | solution.py:17
  153.7 7.6 %all-to-all-done.6 = bf16[8,16,416]{2,1,0:T(8,128)(2,1)S(1)} async-done(((bf16[8,16,416]{2,1,0:T(8,128)(2,1)}), bf16[8,16,416]{2,1,0:T(8,128)(2,1)S(1)}, u32[]{:S(2)}, u32[]{:S(2)}) %all-to-all-start.6) | async-done | bytes 106528 | tf_op jit(solution)/shard_map/all_to_all | solution.py:17
  161.4 0.1 dot_general.32
  161.5 0.3 fusion.10
  161.8 1.5 select_bitcast_fusion.1
  163.2 0.1 pad_maximum_fusion.5
  163.3 0.5 copy.13
  163.9 32.1 %all_to_all.42 = bf16[128,2,1024]{2,1,0:T(2,128)(2,1)S(1)} all-to-all(bf16[128,2,1024]{2,1,0:T(2,128)(2,1)S(1)} %bitcast.61), channel_id=1, replica_groups=mesh['hid'=64,'z'=8,'core'=2] {'hid','core'}, dimensions={0} | all-to-all | bytes 1048576 | tf_op jit(solution)/shard_map/all_to_all | solution.py:17
  196.0 0.2 reshape.70
  196.2 0.8 reduce_sum.45
  (18 shorter events, 0.2 us)
Async XLA Ops:
  0.0 19.6 %copy-start.5 = (bf16[4,1024]{1,0:T(4,128)(2,1)S(1)}, bf16[4,1024]{1,0:T(4,128)(2,1)}, u32[]{:S(2)}) copy-start(bf16[4,1024]{1,0:T(4,128)(2,1)} %param.4) | copy-start | bytes 24580
  3.4 42.8 %copy-start.1 = (bf16[1024,416]{0,1:T(8,128)(2,1)S(1)}, bf16[1024,416]{0,1:T(8,128)(2,1)}, u32[]{:S(2)}) copy-start(bf16[1024,416]{0,1:T(8,128)(2,1)} %param.6) | copy-start | bytes 2555908
  3.4 42.8 %copy-start.2 = (bf16[1024,416]{0,1:T(8,128)(2,1)S(1)}, bf16[1024,416]{0,1:T(8,128)(2,1)}, u32[]{:S(2)}) copy-start(bf16[1024,416]{0,1:T(8,128)(2,1)} %param.5) | copy-start | bytes 2555908
  3.4 43.5 %collective-permute-start = (bf16[1248,1024]{1,0:T(8,128)(2,1)}, bf16[1248,1024]{1,0:T(8,128)(2,1)}, u32[]{:S(2)}, u32[]{:S(2)}) collective-permute-start(bf16[1248,1024]{1,0:T(8,128)(2,1)} %pad_maximum_fusion), channel_id=1, source_target_pairs={{0,1},{1,0},{2,3},{3,2},{4,5},{5,4},{6,7},{7,6},{8,9},{9,8},{10,11... | collective-permute-start | bytes 7667720 | tf_op jit(solution)/shard_map/ppermute | solution.py:30
  20.7 24.8 %all-to-all-start = ((bf16[128,2,1024]{2,1,0:T(2,128)(2,1)}), bf16[128,2,1024]{2,1,0:T(2,128)(2,1)S(1)}, u32[]{:S(2)}, u32[]{:S(2)}) async-start(bf16[128,2,1024]{2,1,0:T(2,128)(2,1)} %bitcast), calls=%async_computation | async-start | bytes 1048576 | tf_op jit(solution)/shard_map/all_to_all | solution.py:17
  46.9 34.1 %copy-start = (bf16[416,1024]{1,0:T(8,128)(2,1)S(1)}, bf16[416,1024]{1,0:T(8,128)(2,1)}, u32[]{:S(2)}) copy-start(bf16[416,1024]{1,0:T(8,128)(2,1)} %param.7) | copy-start | bytes 2555908
  84.0 23.2 %all-to-all-start.3 = ((bf16[64,2,2048]{2,1,0:T(2,128)(2,1)}), bf16[64,2,2048]{2,1,0:T(2,128)(2,1)S(1)}, u32[]{:S(2)}, u32[]{:S(2)}) async-start(bf16[64,2,2048]{2,1,0:T(2,128)(2,1)} %reshape.66), calls=%async_computation.3 | async-start | bytes 1048576 | tf_op jit(solution)/shard_map/all_to_all | solution.py:17
  107.6 24.9 %copy-start.3 = (bf16[1024,416]{0,1:T(8,128)(2,1)S(1)}, bf16[1024,416]{0,1:T(8,128)(2,1)}, u32[]{:S(2)}) copy-start(bf16[1024,416]{0,1:T(8,128)(2,1)} %param.5) | copy-start | bytes 2555908
  108.7 22.8 %all-to-all-start.4 = ((bf16[64,2,2048]{2,1,0:T(2,128)(2,1)}), bf16[64,2,2048]{2,1,0:T(2,128)(2,1)S(1)}, u32[]{:S(2)}, u32[]{:S(2)}) async-start(bf16[64,2,2048]{2,1,0:T(2,128)(2,1)} %broadcast_in_dim.63), calls=%async_computation.4 | async-start | bytes 1048576 | tf_op jit(solution)/shard_map/all_to_all | solution.py:17
  132.5 1.6 copy-start.4
  137.1 12.3 %all-to-all-start.5 = ((bf16[8,16,832]{2,1,0:T(8,128)(2,1)}), bf16[8,16,832]{2,1,0:T(8,128)(2,1)S(1)}, u32[]{:S(2)}, u32[]{:S(2)}) async-start(bf16[8,16,832]{2,1,0:T(8,128)(2,1)} %bitcast.13), calls=%async_computation.5 | async-start | bytes 458752 | tf_op jit(solution)/shard_map/all_to_all | solution.py:17
  150.2 11.2 %all-to-all-start.6 = ((bf16[8,16,416]{2,1,0:T(8,128)(2,1)}), bf16[8,16,416]{2,1,0:T(8,128)(2,1)S(1)}, u32[]{:S(2)}, u32[]{:S(2)}) async-start(bf16[8,16,416]{2,1,0:T(8,128)(2,1)} %broadcast_in_dim.64), calls=%async_computation.6 | async-start | bytes 262144 | tf_op jit(solution)/shard_map/all_to_all | solution.py:17

commit v3 on v2

v3 whole, which is shorter than its diff:
```python
import functools

import jax
import jax.numpy as jnp
from jax import lax
from jax.experimental import pallas as pl
from jax.experimental.pallas import tpu as pltpu
from jax.sharding import Mesh, PartitionSpec as P

STEPS = 2
CORES = 2
BLOCKS = 8
F32, BF16 = jnp.float32, jnp.bfloat16
VMEM_BYTES = 16 * 2**20


def dot(a, b):
    return jnp.dot(a, b, preferred_element_type=F32)


def dot_t(a, b):
    return lax.dot_general(a, b, (((1,), (1,)), ((), ())), preferred_element_type=F32)


def kernel_call(body, out_shape, n_in, scalars=False):
    vmem = pl.BlockSpec(memory_space=pltpu.VMEM)
    specs = [pl.BlockSpec(memory_space=pltpu.SMEM)] if scalars else []
    single = not isinstance(out_shape, (list, tuple))
    return pl.pallas_call(
        body,
        out_shape=out_shape,
        in_specs=specs + [vmem] * n_in,
        out_specs=vmem if single else [vmem] * len(out_shape),
        compiler_params=pltpu.CompilerParams(vmem_limit_bytes=VMEM_BYTES),
    )


def store_partial(out, gate, up):
    n, two, units = out.shape
    out[:, : two // 2, :] = gate.astype(BF16).reshape(n, two // 2, units)
    out[:, two // 2 :, :] = up.astype(BF16).reshape(n, two // 2, units)


def first_products(here, there, gate, up, gate_there, up_there, out):
    x, y = here[...], there[...]
    store_partial(
        out,
        dot_t(x, gate[...]) + dot_t(y, gate_there[...]),
        dot_t(x, up[...]) + dot_t(y, up_there[...]),
    )


def block_products(blocks, gate, up, gate_there, up_there, out):
    n_rows, n_cols, rows, cols = blocks.shape
    x = jnp.concatenate(
        [blocks[:, k].reshape(n_rows * rows, cols) for k in range(n_cols)], axis=1
    )
    span = n_cols // 2 * cols
    x, y = x[:, :span], x[:, span:]
    store_partial(
        out,
        dot_t(x, gate[...]) + dot_t(y, gate_there[...]),
        dot_t(x, up[...]) + dot_t(y, up_there[...]),
    )


def activation(parts, out):
    total = parts[0].astype(F32)
    for k in range(1, parts.shape[0]):
        total += parts[k].astype(F32)
    rows = total.shape[0] // 2
    gate, up = total[:rows], total[rows:]
    hidden = (gate / (1.0 + jnp.exp(-gate)) * up).astype(BF16)
    for k in range(out.shape[0]):
        out[k] = hidden


def down_blocks(hidden, down, down_there, out):
    n_rows, n_cols, rows, cols = out.shape
    x = hidden[...].reshape(n_rows * rows, hidden.shape[-1])
    for half, weight in enumerate((down, down_there)):
        for k in range(n_cols // 2):
            value = dot(x, weight[:, k * cols : (k + 1) * cols])
            out[:, half * (n_cols // 2) + k] = value.astype(BF16).reshape(n_rows, rows, cols)


def add_branch(parts, block, out, copies):
    total = parts[0].astype(F32)
    for k in range(1, parts.shape[0]):
        total += parts[k].astype(F32)
    stream = (block[...].astype(F32) + total).astype(BF16)
    out[...] = stream
    for k in range(copies.shape[0]):
        copies[k] = stream


def last_down(place, hidden, down, block, out):
    n, rows, units = hidden.shape
    total, cols = n * rows, block.shape[1]

    def source(width):
        row = lax.broadcasted_iota(jnp.int32, (total, width), 0)
        group, inner = row & ~(CORES * rows - 1), row & (CORES * rows - 1)
        pair = CORES * (rows // BLOCKS)
        owner, within = inner // pair, inner % pair
        return group + within // (pair // CORES) * rows + owner * (pair // CORES) + within % (pair // CORES)

    order = source(total) == lax.broadcasted_iota(jnp.int32, (total, total), 1)
    x = dot(order.astype(F32).astype(BF16), hidden[...].reshape(total, units)).astype(BF16)
    own_rows = source(rows) == lax.broadcasted_iota(jnp.int32, (total, rows), 1) + place[0] * rows
    addend = dot(own_rows.astype(F32).astype(BF16), block[...])
    for k in range(out.shape[1] // cols):
        value = dot(x, down[:, k * cols : (k + 1) * cols])
        value += jnp.where(place[1] == k, addend, 0.0)
        out[:, k * cols : (k + 1) * cols] = value.astype(BF16)


def exchange(parts, axes):
    return lax.all_to_all(parts, axes, 0, 0, tiled=True)


def per_device(tokens, gate, up, down):
    n_hid, n_z = lax.axis_size("hid"), lax.axis_size("z")
    own, span = tokens.shape
    units = gate.shape[1]
    half = own // CORES
    rows = n_hid * half
    chunk = rows // n_z
    block_rows, block_cols = rows // BLOCKS, CORES * span // BLOCKS
    core, hid = lax.axis_index("core"), lax.axis_index("hid")
    first = core == 0
    row_block, col_block = hid // BLOCKS, hid % BLOCKS
    in_own = col_block < BLOCKS // 2
    col_start = col_block % (BLOCKS // 2) * block_cols

    swap = functools.partial(lax.ppermute, axis_name="core", perm=[(0, 1), (1, 0)])
    gate, up = gate.T, up.T
    weights = (gate, up, swap(gate), swap(up))
    down_there = swap(down)

    copies = jnp.broadcast_to(tokens.reshape(1, CORES, half, span), (n_hid, CORES, half, span))
    gathered = exchange(copies.reshape(n_hid * CORES, half, span), ("hid", "core"))
    gathered = gathered.reshape(n_hid, CORES, half, span)
    low, high = gathered[:, 0], gathered[:, 1]
    here = jnp.where(first, low, high).reshape(rows, span)
    there = jnp.where(first, high, low).reshape(rows, span)
    start = (row_block * block_rows, col_start)
    size = (block_rows, block_cols)
    block = jnp.where(
        in_own, lax.dynamic_slice(here, start, size), lax.dynamic_slice(there, start, size)
    )

    partial_shape = jax.ShapeDtypeStruct((n_z, 2 * chunk, units), BF16)
    partial_value = kernel_call(first_products, partial_shape, 6)(here, there, *weights)
    for repeat in range(STEPS):
        last = repeat == STEPS - 1
        parts = exchange(partial_value, "z")
        n_copies = n_z * CORES if last else n_z
        hidden_shape = jax.ShapeDtypeStruct((n_copies, chunk, units), BF16)
        hidden = kernel_call(activation, hidden_shape, 1)(parts)
        hidden = exchange(hidden, ("z", "core") if last else "z")
        if last:
            break
        blocks_shape = jax.ShapeDtypeStruct((BLOCKS, BLOCKS, block_rows, block_cols), BF16)
        down_part = kernel_call(down_blocks, blocks_shape, 3)(hidden, down, down_there)
        parts = exchange(down_part.reshape(n_hid, block_rows, block_cols), "hid")
        block, copies = kernel_call(
            add_branch,
            [
                jax.ShapeDtypeStruct((block_rows, block_cols), BF16),
                jax.ShapeDtypeStruct((n_hid, block_rows, block_cols), BF16),
            ],
            2,
        )(parts, block)
        blocks = exchange(copies, "hid").reshape(blocks_shape.shape)
        partial_value = kernel_call(block_products, partial_shape, 5)(blocks, *weights)

    block = jnp.where(in_own, block, swap(block))
    block_core = jnp.where(in_own, core, 1 - core)
    place = jnp.stack([row_block * CORES + block_core, col_block % (BLOCKS // 2)]).astype(jnp.int32)
    branch = kernel_call(last_down, jax.ShapeDtypeStruct((CORES * rows, span), BF16), 3, True)(
        place, hidden, down, block
    )
    parts = exchange(branch.reshape(n_hid, own, span), "hid")
    return jnp.sum(parts.astype(F32), axis=0).astype(BF16)


def solution(mesh):
    n_hid, n_wid = mesh.devices.shape
    fine = Mesh(mesh.devices.reshape(n_hid, n_wid // CORES, CORES), ("hid", "z", "core"))
    wid = ("z", "core")
    in_specs = (P("hid", wid), P(wid, "hid"), P(wid, "hid"), P("hid", wid))
    out_specs = P("hid", wid)
    return jax.shard_map(
        per_device, mesh=fine, in_specs=in_specs, out_specs=out_specs, check_vma=False
    )
```

time: 198 us -> 199 us (level)
  waiting for transfers between devices: 66.2 us -> 44.4 us
  blocking collectives: 63.8 us -> 80.8 us
  matrix products: 10 us -> 0 us
  Pallas kernels: 0 us -> 9.27 us
  starting transfers between devices: 43.5 us -> 49.3 us
  local copies, waits for them, and re-layouts: 7.05 us -> 9.66 us
  other arithmetic: 6.15 us -> 4.06 us
    all_to_all x5 -> x4, waiting for transfers between devices: 66.2 us -> 43.5 us  [exchange(): return lax.all_to_all(parts, axes, 0, 0, tiled=True)]
    all_to_all x3 -> x4, blocking collectives: 63.8 us -> 80.8 us  [exchange(): return lax.all_to_all(parts, axes, 0, 0, tiled=True)]
    all_to_all x5 -> x4, starting transfers between devices: 27.3 us -> 40 us  [exchange(): return lax.all_to_all(parts, axes, 0, 0, tiled=True)]
    dot_general x8 -> x0, matrix products: 10 us -> none  [the longest x4 6.45 us: product(): lax.dot_general(rows, weight, (((1,), (1,)), ((), ())), preferred_element...]
    pallas_call x0 -> x7, Pallas kernels: none -> 9.27 us  [the longest x1 2.28 us: per_device(): kernel_call(first_products, partial_shape, 6)(here, there, *weights)]
    ppermute x1 -> x4, starting transfers between devices: 16.2 us -> 9.39 us  [the longest x2 4.84 us: per_device(): weights = (gate, up, swap(gate), swap(up))]
    unnamed x12 -> x16, local copies, waits for them, and re-layouts: 0.03 us -> 4.13 us
    concatenate x2 -> x0, other arithmetic: 3.45 us -> none  [the longest x1 3.41 us: per_device(): weights = jnp.concatenate([gate_weight.T, up_weight.T, down_weight], axis=0)]
  transfers between devices with their start and end apart: 6 -> 8, of which waited for: 5 -> 5; matrix products, arithmetic and copies ran while one was open for 2% -> 3% of each run, Pallas kernels for 0% -> 1%
where the time goes in v3:
time: 199 us; the launch traced here: 198 us
  blocking collectives  80.8 us (41%)
  starting transfers between devices  49.3 us (25%)
  waiting for transfers between devices  44.4 us (22%)
  local copies, waits for them, and re-layouts  9.66 us (5%)
  Pallas kernels  9.27 us (5%)
  other arithmetic  4.06 us (2%)
    all_to_all x4, blocking collectives, exchange(): return lax.all_to_all(parts, axes, 0, 0, tiled=True)  80.8 us
    all_to_all x4, waiting for transfers between devices, exchange(): return lax.all_to_all(parts, axes, 0, 0, tiled=True)  43.5 us
    all_to_all x4, starting transfers between devices, exchange(): return lax.all_to_all(parts, axes, 0, 0, tiled=True)  40 us
    ppermute x2, starting transfers between devices, per_device(): weights = (gate, up, swap(gate), swap(up))  4.84 us
    unnamed x16, local copies, waits for them, and re-layouts  4.13 us
  transfers between devices with their start and end apart: 8, of which 5 were waited for; matrix products, arithmetic and copies ran while one was open for 3% of the time, Pallas kernels for 1%

profile of v3, /device:TPU:1, one launch (start us, length us, event | category | flops | bytes accessed | tf_op | source)
XLA Modules:
  0.0 197.7 jit_solution(1875541081678561715)
XLA Ops:
  0.0 0.0 copy-start
  0.0 0.8 broadcast_in_dim.7
  0.8 1.1 broadcast_in_dim.8
  1.9 19.3 %all-to-all-start = ((bf16[128,2,1024]{2,1,0:T(2,128)(2,1)}), bf16[128,2,1024]{2,1,0:T(2,128)(2,1)S(1)}, u32[]{:S(2)}, u32[]{:S(2)}) async-start(bf16[128,2,1024]{2,1,0:T(2,128)(2,1)} %bitcast.2), calls=%async_computation | async-start | bytes 1048576 | tf_op jit(solution)/shard_map/all_to_all | solution.py:119
  21.2 2.9 %collective-permute-start = (bf16[416,1024]{1,0:T(8,128)(2,1)}, bf16[416,1024]{1,0:T(8,128)(2,1)S(1)}, u32[]{:S(2)}, u32[]{:S(2)}) collective-permute-start(bf16[416,1024]{1,0:T(8,128)(2,1)} %bitcast.8), channel_id=1, source_target_pairs={{0,1},{1,0},{2,3},{3,2},{4,5},{5,4},{6,7},{7,6},{8,9},{9,8},{10,11... | collective-permute-start | bytes 2555912 | tf_op jit(solution)/shard_map/ppermute | solution.py:138
  24.1 1.9 collective-permute-start.1
  26.0 0.0 copy-done
  26.0 2.4 %collective-permute-start.2 = (bf16[416,1024]{1,0:T(8,128)(2,1)S(1)}, bf16[416,1024]{1,0:T(8,128)(2,1)}, u32[]{:S(2)}, u32[]{:S(2)}) collective-permute-start(bf16[416,1024]{1,0:T(8,128)(2,1)S(1)} %copy-done), channel_id=1, source_target_pairs={{0,1},{1,0},{2,3},{3,2},{4,5},{5,4},{6,7},{7,6},{8,9},{9,8},{10,11... | collective-permute-start | bytes 2555912 | tf_op jit(solution)/shard_map/ppermute | solution.py:139
  28.5 12.3 %all-to-all-done = bf16[128,2,1024]{2,1,0:T(2,128)(2,1)S(1)} async-done(((bf16[128,2,1024]{2,1,0:T(2,128)(2,1)}), bf16[128,2,1024]{2,1,0:T(2,128)(2,1)S(1)}, u32[]{:S(2)}, u32[]{:S(2)}) %all-to-all-start) | async-done | bytes 524320 | tf_op jit(solution)/shard_map/all_to_all | solution.py:119
  40.7 0.8 copy-done.7
  41.5 2.4 %broadcast_select_fusion = (bf16[64,1,2,1024]{3,2,1,0:T(2,128)(2,1)}, bf16[64,1,2,1024]{3,2,1,0:T(2,128)(2,1)}) fusion(pred[]{:T(512)S(6)} %eq.7, bf16[64,2,2,1024]{3,2,1,0:T(2,128)(2,1)} %bitcast.16), kind=kLoop, calls=%fused_computation | loop fusion | flops 262144 | bytes 1048577 | tf_op jit(solution)/shard_map/jit(_where)/select_n | solution.py:146
  43.9 1.7 select_n.68.there
  45.7 1.8 select_n.66.here
  47.4 0.0 collective-permute-done.gate_there
  47.4 0.0 collective-permute-done.1.up_there
  47.4 0.0 copy-done.1
  47.4 0.0 copy-done.2
  47.5 0.0 copy-start.4
  47.5 0.9 copy-done.4
  48.4 0.9 copy-done.5
  49.4 2.3 %shard_map.46 = bf16[8,32,416]{2,1,0:T(8,128)(2,1)S(1)} custom-call(bf16[128,1024]{1,0:T(8,128)(2,1)S(1)} %copy-done.5, bf16[128,1024]{1,0:T(8,128)(2,1)S(1)} %copy-done.4, bf16[416,1024]{1,0:T(8,128)(2,1)S(1)} %bitcast.9, bf16[416,1024]{1,0:T(8,128)(2,1)S(1)} %bitcast.12, bf16[416,1024]{1,0:T(8,128)(2,1)S(1)} %collective-permute-done.gate_there, ...), custom_call_target="tpu_custom_call" | custom-call | tf_op jit(solution)/shard_map/pallas_call | solution.py:154
  51.7 21.5 %all_to_all.40.parts = bf16[8,32,416]{2,1,0:T(8,128)(2,1)S(1)} all-to-all(bf16[8,32,416]{2,1,0:T(8,128)(2,1)S(1)} %shard_map.46), channel_id=1, replica_groups=mesh['hid'=64,'z'=8,'core'=2] {'z'}, dimensions={0} | all-to-all | bytes 425984 | tf_op jit(solution)/shard_map/all_to_all | solution.py:119
  73.2 0.1 shard_map.47
  73.2 0.0 copy-start.6
  73.3 0.6 copy-done.6
  73.9 3.4 %all-to-all-start.2 = ((bf16[8,16,416]{2,1,0:T(8,128)(2,1)}), bf16[8,16,416]{2,1,0:T(8,128)(2,1)S(1)}, u32[]{:S(2)}, u32[]{:S(2)}) async-start(bf16[8,16,416]{2,1,0:T(8,128)(2,1)} %copy-done.6), calls=%async_computation.2 | async-start | bytes 262144 | tf_op jit(solution)/shard_map/all_to_all | solution.py:119
  77.3 0.0 collective-permute-done.2.down_there
  77.3 7.9 %all-to-all-done.2.hidden = bf16[8,16,416]{2,1,0:T(8,128)(2,1)S(1)} async-done(((bf16[8,16,416]{2,1,0:T(8,128)(2,1)}), bf16[8,16,416]{2,1,0:T(8,128)(2,1)S(1)}, u32[]{:S(2)}, u32[]{:S(2)}) %all-to-all-start.2) | async-done | bytes 106528 | tf_op jit(solution)/shard_map/all_to_all | solution.py:119
  85.2 1.6 shard_map.48
  86.8 0.0 copy-start.3
  86.8 0.8 copy-done.3
  87.6 8.1 %all-to-all-start.3 = ((bf16[64,16,256]{2,1,0:T(8,128)(2,1)}), bf16[64,16,256]{2,1,0:T(8,128)(2,1)}, u32[]{:S(2)}, u32[]{:S(2)}) async-start(bf16[64,16,256]{2,1,0:T(8,128)(2,1)} %bitcast.14), calls=%async_computation.3 | async-start | bytes 1048576 | tf_op jit(solution)/shard_map/all_to_all | solution.py:119
  95.8 0.7 dynamic-slice_select_fusion.block
  96.5 14.5 %all-to-all-done.3.parts = bf16[64,16,256]{2,1,0:T(8,128)(2,1)} async-done(((bf16[64,16,256]{2,1,0:T(8,128)(2,1)}), bf16[64,16,256]{2,1,0:T(8,128)(2,1)}, u32[]{:S(2)}, u32[]{:S(2)}) %all-to-all-start.3) | async-done | bytes 524320 | tf_op jit(solution)/shard_map/all_to_all | solution.py:119
  111.0 1.2 shard_map.49
  112.2 23.0 %all_to_all.41 = bf16[64,16,256]{2,1,0:T(8,128)(2,1)S(1)} all-to-all(bf16[64,16,256]{2,1,0:T(8,128)(2,1)S(1)} %get-tuple-element.7), channel_id=1, replica_groups=mesh['hid'=64,'z'=8,'core'=2] {'hid'}, dimensions={0} | all-to-all | bytes 1048576 | tf_op jit(solution)/shard_map/all_to_all | solution.py:119
  135.2 2.3 %shard_map.50 = bf16[8,32,416]{2,1,0:T(8,128)(2,1)S(1)} custom-call(bf16[8,8,16,256]{3,2,1,0:T(8,128)(2,1)S(1)} %bitcast.15, bf16[416,1024]{1,0:T(8,128)(2,1)S(1)} %bitcast.10, bf16[416,1024]{1,0:T(8,128)(2,1)S(1)} %bitcast.13, bf16[416,1024]{1,0:T(8,128)(2,1)S(1)} %collective-permute-done.gate_there, bf16[416,1024]{1,0:T(8,128)(2,1)} %collective-permute-done.1.up_there), custom_call_target="tpu_custom_call" | custom-call | tf_op jit(solution)/shard_map/pallas_call | solution.py:176
  137.4 12.5 %all_to_all.42.parts = bf16[8,32,416]{2,1,0:T(8,128)(2,1)S(1)} all-to-all(bf16[8,32,416]{2,1,0:T(8,128)(2,1)S(1)} %shard_map.50), channel_id=1, replica_groups=mesh['hid'=64,'z'=8,'core'=2] {'z'}, dimensions={0} | all-to-all | bytes 425984 | tf_op jit(solution)/shard_map/all_to_all | solution.py:119
  149.9 0.8 shard_map.51
  150.7 9.2 %all-to-all-start.6 = ((bf16[16,16,416]{2,1,0:T(8,128)(2,1)}), bf16[16,16,416]{2,1,0:T(8,128)(2,1)S(1)}, u32[]{:S(2)}, u32[]{:S(2)}) async-start(bf16[16,16,416]{2,1,0:T(8,128)(2,1)} %shard_map.51), calls=%async_computation.6 | async-start | bytes 524288 | tf_op jit(solution)/shard_map/all_to_all | solution.py:119
  159.9 2.1 %collective-permute-start.3 = (bf16[16,256]{1,0:T(8,128)(2,1)S(1)}, bf16[16,256]{1,0:T(8,128)(2,1)S(1)}, u32[]{:S(2)}, u32[]{:S(2)}) collective-permute-start(bf16[16,256]{1,0:T(8,128)(2,1)S(1)} %get-tuple-element.8), channel_id=1, source_target_pairs={{0,1},{1,0},{2,3},{3,2},{4,5},{5,4},{6,7},{7,6},{8,9},{9,8},{10,11... | collective-permute-start | bytes 24584 | tf_op jit(solution)/shard_map/ppermute | solution.py:178
  162.0 0.1 pad_add_fusion.place
  162.1 0.8 collective-permute-done.3
  162.9 8.8 %all-to-all-done.6.hidden = bf16[16,16,416]{2,1,0:T(8,128)(2,1)S(1)} async-done(((bf16[16,16,416]{2,1,0:T(8,128)(2,1)}), bf16[16,16,416]{2,1,0:T(8,128)(2,1)S(1)}, u32[]{:S(2)}, u32[]{:S(2)}) %all-to-all-start.6) | async-done | bytes 213024 | tf_op jit(solution)/shard_map/all_to_all | solution.py:119
  171.7 1.1 shard_map.52
  172.9 0.2 reshape.31
  173.1 23.7 %all_to_all.43 = bf16[64,4,1024]{2,1,0:T(4,128)(2,1)S(1)} all-to-all(bf16[64,4,1024]{2,1,0:T(4,128)(2,1)S(1)} %reshape.31), channel_id=1, replica_groups=mesh['hid'=64,'z'=8,'core'=2] {'hid'}, dimensions={0} | all-to-all | bytes 1048576 | tf_op jit(solution)/shard_map/all_to_all | solution.py:119
  196.8 0.8 reduce_sum.12
  (5 shorter events, 0.0 us)
Async XLA Ops:
  0.0 26.0 %copy-start = (bf16[416,1024]{1,0:T(8,128)(2,1)S(1)}, bf16[416,1024]{1,0:T(8,128)(2,1)}, u32[]{:S(2)}) copy-start(bf16[416,1024]{1,0:T(8,128)(2,1)} %down.3) | copy-start | bytes 2555908
  1.9 38.9 %all-to-all-start = ((bf16[128,2,1024]{2,1,0:T(2,128)(2,1)}), bf16[128,2,1024]{2,1,0:T(2,128)(2,1)S(1)}, u32[]{:S(2)}, u32[]{:S(2)}) async-start(bf16[128,2,1024]{2,1,0:T(2,128)(2,1)} %bitcast.2), calls=%async_computation | async-start | bytes 1048576 | tf_op jit(solution)/shard_map/all_to_all | solution.py:119
  21.2 26.3 %collective-permute-start = (bf16[416,1024]{1,0:T(8,128)(2,1)}, bf16[416,1024]{1,0:T(8,128)(2,1)S(1)}, u32[]{:S(2)}, u32[]{:S(2)}) collective-permute-start(bf16[416,1024]{1,0:T(8,128)(2,1)} %bitcast.8), channel_id=1, source_target_pairs={{0,1},{1,0},{2,3},{3,2},{4,5},{5,4},{6,7},{7,6},{8,9},{9,8},{10,11... | collective-permute-start | bytes 2555912 | tf_op jit(solution)/shard_map/ppermute | solution.py:138
  24.1 23.4 %collective-permute-start.1 = (bf16[416,1024]{1,0:T(8,128)(2,1)}, bf16[416,1024]{1,0:T(8,128)(2,1)}, u32[]{:S(2)}, u32[]{:S(2)}) collective-permute-start(bf16[416,1024]{1,0:T(8,128)(2,1)} %bitcast.11), channel_id=1, source_target_pairs={{0,1},{1,0},{2,3},{3,2},{4,5},{5,4},{6,7},{7,6},{8,9},{9,8},{10,11... | collective-permute-start | bytes 2555912 | tf_op jit(solution)/shard_map/ppermute | solution.py:138
  26.0 51.2 %collective-permute-start.2 = (bf16[416,1024]{1,0:T(8,128)(2,1)S(1)}, bf16[416,1024]{1,0:T(8,128)(2,1)}, u32[]{:S(2)}, u32[]{:S(2)}) collective-permute-start(bf16[416,1024]{1,0:T(8,128)(2,1)S(1)} %copy-done), channel_id=1, source_target_pairs={{0,1},{1,0},{2,3},{3,2},{4,5},{5,4},{6,7},{7,6},{8,9},{9,8},{10,11... | collective-permute-start | bytes 2555912 | tf_op jit(solution)/shard_map/ppermute | solution.py:139
  40.7 0.8 copy-start.7
  41.5 5.9 %copy-start.1 = (bf16[1024,416]{0,1:T(8,128)(2,1)S(1)}, bf16[1024,416]{0,1:T(8,128)(2,1)}, u32[]{:S(2)}) copy-start(bf16[1024,416]{0,1:T(8,128)(2,1)} %param.5) | copy-start | bytes 2555908
  41.5 5.9 %copy-start.2 = (bf16[1024,416]{0,1:T(8,128)(2,1)S(1)}, bf16[1024,416]{0,1:T(8,128)(2,1)}, u32[]{:S(2)}) copy-start(bf16[1024,416]{0,1:T(8,128)(2,1)} %param.6) | copy-start | bytes 2555908
  47.5 1.0 copy-start.4
  48.4 0.9 copy-start.5
  73.2 0.7 copy-start.6
  73.9 11.3 %all-to-all-start.2 = ((bf16[8,16,416]{2,1,0:T(8,128)(2,1)}), bf16[8,16,416]{2,1,0:T(8,128)(2,1)S(1)}, u32[]{:S(2)}, u32[]{:S(2)}) async-start(bf16[8,16,416]{2,1,0:T(8,128)(2,1)} %copy-done.6), calls=%async_computation.2 | async-start | bytes 262144 | tf_op jit(solution)/shard_map/all_to_all | solution.py:119
  86.8 0.8 copy-start.3
  87.6 23.4 %all-to-all-start.3 = ((bf16[64,16,256]{2,1,0:T(8,128)(2,1)}), bf16[64,16,256]{2,1,0:T(8,128)(2,1)}, u32[]{:S(2)}, u32[]{:S(2)}) async-start(bf16[64,16,256]{2,1,0:T(8,128)(2,1)} %bitcast.14), calls=%async_computation.3 | async-start | bytes 1048576 | tf_op jit(solution)/shard_map/all_to_all | solution.py:119
  150.7 21.0 %all-to-all-start.6 = ((bf16[16,16,416]{2,1,0:T(8,128)(2,1)}), bf16[16,16,416]{2,1,0:T(8,128)(2,1)S(1)}, u32[]{:S(2)}, u32[]{:S(2)}) async-start(bf16[16,16,416]{2,1,0:T(8,128)(2,1)} %shard_map.51), calls=%async_computation.6 | async-start | bytes 524288 | tf_op jit(solution)/shard_map/all_to_all | solution.py:119
  159.9 3.1 %collective-permute-start.3 = (bf16[16,256]{1,0:T(8,128)(2,1)S(1)}, bf16[16,256]{1,0:T(8,128)(2,1)S(1)}, u32[]{:S(2)}, u32[]{:S(2)}) collective-permute-start(bf16[16,256]{1,0:T(8,128)(2,1)S(1)} %get-tuple-element.8), channel_id=1, source_target_pairs={{0,1},{1,0},{2,3},{3,2},{4,5},{5,4},{6,7},{7,6},{8,9},{9,8},{10,11... | collective-permute-start | bytes 24584 | tf_op jit(solution)/shard_map/ppermute | solution.py:178

commit v4 on v3

--- a/solution.py
+++ b/solution.py
@@ -22,7 +22,7 @@
     return lax.dot_general(a, b, (((1,), (1,)), ((), ())), preferred_element_type=F32)
 
 
-def kernel_call(body, out_shape, n_in, scalars=False):
+def kernel_call(body, out_shape, n_in, scalars=False, scratch=()):
     vmem = pl.BlockSpec(memory_space=pltpu.VMEM)
     specs = [pl.BlockSpec(memory_space=pltpu.SMEM)] if scalars else []
     single = not isinstance(out_shape, (list, tuple))
@@ -31,6 +31,7 @@
         out_shape=out_shape,
         in_specs=specs + [vmem] * n_in,
         out_specs=vmem if single else [vmem] * len(out_shape),
+        scratch_shapes=scratch,
         compiler_params=pltpu.CompilerParams(vmem_limit_bytes=VMEM_BYTES),
     )
 
@@ -41,8 +42,46 @@
     out[:, two // 2 :, :] = up.astype(BF16).reshape(n, two // 2, units)
 
 
-def first_products(here, there, gate, up, gate_there, up_there, out):
-    x, y = here[...], there[...]
+def copy_tokens(tokens, out):
+    n, cores, lines, cols = out.shape
+    half = tokens.shape[0] // cores
+    values = tokens[...].astype(F32)
+    for c in range(cores):
+        block = jnp.concatenate(
+            [
+                values[c * half + j : c * half + j + 1, k * cols : (k + 1) * cols]
+                for j in range(half)
+                for k in range(lines // half)
+            ],
+            axis=0,
+        ).astype(BF16)
+        for h in range(n):
+            out[h, c] = block
+
+
+def first_products(place, gathered, gate, up, gate_there, up_there, out, block, stream):
+    n_hid, cores, lines, cols = gathered.shape
+    n_blocks, rows, _ = stream.shape
+    half, parts = rows // n_hid, n_blocks // cores
+    owners = min(n_hid, 256 // lines)
+    size = owners * lines
+    line = lax.broadcasted_iota(jnp.int32, (size, size), 0)
+    k, row = line // (owners * half), line % (owners * half)
+    source = row // half * lines + row % half * parts + k
+    order = (source == lax.broadcasted_iota(jnp.int32, (size, size), 1)).astype(F32).astype(BF16)
+    for which in range(cores):
+        core = place[0] if which == 0 else 1 - place[0]
+        for group in range(n_hid // owners):
+            piece = gathered[pl.ds(group * owners, owners), core].reshape(size, cols)
+            sorted_piece = dot(order, piece).astype(BF16).reshape(parts, owners * half, cols)
+            start = group * owners * half
+            stream[which * parts : (which + 1) * parts, start : start + owners * half] = sorted_piece
+    size = block.shape[0]
+    block[...] = stream[place[2], pl.ds(pl.multiple_of(place[1] * size, size), size), :]
+    x, y = (
+        jnp.concatenate([stream[which * parts + k] for k in range(parts)], axis=1)
+        for which in range(cores)
+    )
     store_partial(
         out,
         dot_t(x, gate[...]) + dot_t(y, gate_there[...]),
@@ -128,30 +167,31 @@
     chunk = rows // n_z
     block_rows, block_cols = rows // BLOCKS, CORES * span // BLOCKS
     core, hid = lax.axis_index("core"), lax.axis_index("hid")
-    first = core == 0
     row_block, col_block = hid // BLOCKS, hid % BLOCKS
     in_own = col_block < BLOCKS // 2
-    col_start = col_block % (BLOCKS // 2) * block_cols
 
     swap = functools.partial(lax.ppermute, axis_name="core", perm=[(0, 1), (1, 0)])
     gate, up = gate.T, up.T
     weights = (gate, up, swap(gate), swap(up))
     down_there = swap(down)
 
-    copies = jnp.broadcast_to(tokens.reshape(1, CORES, half, span), (n_hid, CORES, half, span))
-    gathered = exchange(copies.reshape(n_hid * CORES, half, span), ("hid", "core"))
-    gathered = gathered.reshape(n_hid, CORES, half, span)
-    low, high = gathered[:, 0], gathered[:, 1]
-    here = jnp.where(first, low, high).reshape(rows, span)
-    there = jnp.where(first, high, low).reshape(rows, span)
-    start = (row_block * block_rows, col_start)
-    size = (block_rows, block_cols)
-    block = jnp.where(
-        in_own, lax.dynamic_slice(here, start, size), lax.dynamic_slice(there, start, size)
-    )
-
+    lines = half * span // block_cols
+    copies_shape = jax.ShapeDtypeStruct((n_hid, CORES, lines, block_cols), BF16)
+    copies = kernel_call(copy_tokens, copies_shape, 1)(tokens)
+    gathered = exchange(copies.reshape(n_hid * CORES, lines, block_cols), ("hid", "core"))
     partial_shape = jax.ShapeDtypeStruct((n_z, 2 * chunk, units), BF16)
-    partial_value = kernel_call(first_products, partial_shape, 6)(here, there, *weights)
+    partial_value, block = kernel_call(
+        first_products,
+        [partial_shape, jax.ShapeDtypeStruct((block_rows, block_cols), BF16)],
+        5,
+        True,
+        [pltpu.VMEM((BLOCKS, rows, block_cols), BF16)],
+    )(
+        jnp.stack([core, row_block, col_block]).astype(jnp.int32),
+        gathered.reshape(copies_shape.shape),
+        *weights,
+    )
+    partial_value, down_there = lax.optimization_barrier((partial_value, down_there))
     for repeat in range(STEPS):
         last = repeat == STEPS - 1
         parts = exchange(partial_value, "z")

time: 199 us -> 187 us (0.940)
  blocking collectives: 80.8 us -> 114 us
  waiting for transfers between devices: 44.4 us -> 21.8 us
  starting transfers between devices: 49.3 us -> 38 us
  local copies, waits for them, and re-layouts: 9.66 us -> 3.22 us
  other arithmetic: 4.06 us -> 1 us
    all_to_all x4 -> x6, blocking collectives: 80.8 us -> 114 us  [exchange(): return lax.all_to_all(parts, axes, 0, 0, tiled=True)]
    all_to_all x4 -> x2, waiting for transfers between devices: 43.5 us -> 21 us  [exchange(): return lax.all_to_all(parts, axes, 0, 0, tiled=True)]
    all_to_all x4 -> x2, starting transfers between devices: 40 us -> 28.6 us  [exchange(): return lax.all_to_all(parts, axes, 0, 0, tiled=True)]
    select_n x2 -> x0, local copies, waits for them, and re-layouts: 3.49 us -> none  [the longest x1 1.75 us: per_device(): here = jnp.where(first, low, high).reshape(rows, span)]
    select_n x2 -> x0, other arithmetic: 3.13 us -> none  [the longest x1 2.4 us: per_device(): there = jnp.where(first, high, low).reshape(rows, span)]
    unnamed x16 -> x12, local copies, waits for them, and re-layouts: 4.13 us -> 3.02 us
  transfers between devices with their start and end apart: 8 -> 6, of which waited for: 5 -> 3; matrix products, arithmetic and copies ran while one was open for 3% -> 0% of each run, Pallas kernels for 1% -> 1%
where the time goes in v4:
time: 187 us; the launch traced here: 186 us
  blocking collectives  114 us (61%)
  starting transfers between devices  38 us (20%)
  waiting for transfers between devices  21.8 us (12%)
  Pallas kernels  7.47 us (4%)
  local copies, waits for them, and re-layouts  3.22 us (2%)
    all_to_all x6, blocking collectives, exchange(): return lax.all_to_all(parts, axes, 0, 0, tiled=True)  114 us
    all_to_all x2, starting transfers between devices, exchange(): return lax.all_to_all(parts, axes, 0, 0, tiled=True)  28.6 us
    all_to_all x2, waiting for transfers between devices, exchange(): return lax.all_to_all(parts, axes, 0, 0, tiled=True)  21 us
    ppermute x2, starting transfers between devices, per_device(): weights = (gate, up, swap(gate), swap(up))  4.84 us
  transfers between devices with their start and end apart: 6, of which 3 were waited for; matrix products, arithmetic and copies ran while one was open for 0% of the time, Pallas kernels for 1%

profile of v4, /device:TPU:1, one launch (start us, length us, event | category | flops | bytes accessed | tf_op | source)
XLA Modules:
  0.0 186.0 jit_solution(9925205324960654231)
XLA Ops:
  0.0 0.0 copy-start.5
  0.0 0.7 copy-done.5
  0.7 0.0 copy-start
  0.7 0.8 shard_map.46
  1.5 19.3 %all-to-all-start = ((bf16[128,8,256]{2,1,0:T(8,128)(2,1)}), bf16[128,8,256]{2,1,0:T(8,128)(2,1)S(1)}, u32[]{:S(2)}, u32[]{:S(2)}) async-start(bf16[128,8,256]{2,1,0:T(8,128)(2,1)} %bitcast.5), calls=%async_computation | async-start | bytes 1048576 | tf_op jit(solution)/shard_map/all_to_all | solution.py:158
  20.9 2.9 %collective-permute-start = (bf16[416,1024]{1,0:T(8,128)(2,1)}, bf16[416,1024]{1,0:T(8,128)(2,1)S(1)}, u32[]{:S(2)}, u32[]{:S(2)}) collective-permute-start(bf16[416,1024]{1,0:T(8,128)(2,1)} %bitcast.11), channel_id=1, source_target_pairs={{0,1},{1,0},{2,3},{3,2},{4,5},{5,4},{6,7},{7,6},{8,9},{9,8},{10,11... | collective-permute-start | bytes 2555912 | tf_op jit(solution)/shard_map/ppermute | solution.py:175
  23.8 1.9 %collective-permute-start.1 = (bf16[416,1024]{1,0:T(8,128)(2,1)}, bf16[416,1024]{1,0:T(8,128)(2,1)S(1)}, u32[]{:S(2)}, u32[]{:S(2)}) collective-permute-start(bf16[416,1024]{1,0:T(8,128)(2,1)} %bitcast.14), channel_id=1, source_target_pairs={{0,1},{1,0},{2,3},{3,2},{4,5},{5,4},{6,7},{7,6},{8,9},{9,8},{10,11... | collective-permute-start | bytes 2555912 | tf_op jit(solution)/shard_map/ppermute | solution.py:175
  25.7 0.0 copy-done
  25.7 2.4 %collective-permute-start.2 = (bf16[416,1024]{1,0:T(8,128)(2,1)S(1)}, bf16[416,1024]{1,0:T(8,128)(2,1)}, u32[]{:S(2)}, u32[]{:S(2)}) collective-permute-start(bf16[416,1024]{1,0:T(8,128)(2,1)S(1)} %copy-done), channel_id=1, source_target_pairs={{0,1},{1,0},{2,3},{3,2},{4,5},{5,4},{6,7},{7,6},{8,9},{9,8},{10,11... | collective-permute-start | bytes 2555912 | tf_op jit(solution)/shard_map/ppermute | solution.py:176
  28.2 0.1 pad_add_fusion.1.place
  28.2 0.0 collective-permute-done.gate_there
  28.3 0.0 collective-permute-done.1.up_there
  28.3 12.2 %all-to-all-done = bf16[128,8,256]{2,1,0:T(8,128)(2,1)S(1)} async-done(((bf16[128,8,256]{2,1,0:T(8,128)(2,1)}), bf16[128,8,256]{2,1,0:T(8,128)(2,1)S(1)}, u32[]{:S(2)}, u32[]{:S(2)}) %all-to-all-start) | async-done | bytes 524320 | tf_op jit(solution)/shard_map/all_to_all | solution.py:158
  40.4 0.0 copy-start.1
  40.4 1.2 copy-done.1
  41.6 0.0 copy-start.3
  41.6 1.2 copy-done.3
  42.8 1.8 shard_map.47
  44.6 0.0 collective-permute-done.2.down_there
  44.6 21.5 %all_to_all.40.parts = bf16[8,32,416]{2,1,0:T(8,128)(2,1)S(1)} all-to-all(bf16[8,32,416]{2,1,0:T(8,128)(2,1)S(1)} %get-tuple-element.12), channel_id=1, replica_groups=mesh['hid'=64,'z'=8,'core'=2] {'z'}, dimensions={0} | all-to-all | bytes 425984 | tf_op jit(solution)/shard_map/all_to_all | solution.py:158
  66.2 0.1 shard_map.48
  66.2 10.4 %all_to_all.41.hidden = bf16[8,16,416]{2,1,0:T(8,128)(2,1)S(1)} all-to-all(bf16[8,16,416]{2,1,0:T(8,128)(2,1)S(1)} %shard_map.48), channel_id=1, replica_groups=mesh['hid'=64,'z'=8,'core'=2] {'z'}, dimensions={0} | all-to-all | bytes 212992 | tf_op jit(solution)/shard_map/all_to_all | solution.py:158
  76.6 1.6 shard_map.49
  78.2 0.0 copy-start.4
  78.2 23.3 %all_to_all.42.parts = bf16[64,16,256]{2,1,0:T(8,128)(2,1)S(1)} all-to-all(bf16[64,16,256]{2,1,0:T(8,128)(2,1)S(1)} %bitcast.18), channel_id=1, replica_groups=mesh['hid'=64,'z'=8,'core'=2] {'hid'}, dimensions={0} | all-to-all | bytes 1048576 | tf_op jit(solution)/shard_map/all_to_all | solution.py:158
  101.6 0.0 copy-start.2
  101.6 0.1 shard_map.50
  101.7 22.9 %all_to_all.43 = bf16[64,16,256]{2,1,0:T(8,128)(2,1)S(1)} all-to-all(bf16[64,16,256]{2,1,0:T(8,128)(2,1)S(1)} %get-tuple-element.15), channel_id=1, replica_groups=mesh['hid'=64,'z'=8,'core'=2] {'hid'}, dimensions={0} | all-to-all | bytes 1048576 | tf_op jit(solution)/shard_map/all_to_all | solution.py:158
  124.6 0.0 copy-done.4
  124.6 0.0 copy-done.2
  124.6 1.1 shard_map.51
  125.7 12.5 %all_to_all.44.parts = bf16[8,32,416]{2,1,0:T(8,128)(2,1)S(1)} all-to-all(bf16[8,32,416]{2,1,0:T(8,128)(2,1)S(1)} %shard_map.51), channel_id=1, replica_groups=mesh['hid'=64,'z'=8,'core'=2] {'z'}, dimensions={0} | all-to-all | bytes 425984 | tf_op jit(solution)/shard_map/all_to_all | solution.py:158
  138.2 0.8 shard_map.52
  139.0 9.3 %all-to-all-start.6 = ((bf16[16,16,416]{2,1,0:T(8,128)(2,1)}), bf16[16,16,416]{2,1,0:T(8,128)(2,1)S(1)}, u32[]{:S(2)}, u32[]{:S(2)}) async-start(bf16[16,16,416]{2,1,0:T(8,128)(2,1)} %shard_map.52), calls=%async_computation.6 | async-start | bytes 524288 | tf_op jit(solution)/shard_map/all_to_all | solution.py:158
  148.3 2.2 %collective-permute-start.3 = (bf16[16,256]{1,0:T(8,128)(2,1)S(1)}, bf16[16,256]{1,0:T(8,128)(2,1)S(1)}, u32[]{:S(2)}, u32[]{:S(2)}) collective-permute-start(bf16[16,256]{1,0:T(8,128)(2,1)S(1)} %get-tuple-element.16), channel_id=1, source_target_pairs={{0,1},{1,0},{2,3},{3,2},{4,5},{5,4},{6,7},{7,6},{8,9},{9,8},{10,11... | collective-permute-start | bytes 24584 | tf_op jit(solution)/shard_map/ppermute | solution.py:218
  150.4 0.1 pad_add_fusion.place
  150.5 0.8 collective-permute-done.3
  151.3 8.8 %all-to-all-done.6.hidden = bf16[16,16,416]{2,1,0:T(8,128)(2,1)S(1)} async-done(((bf16[16,16,416]{2,1,0:T(8,128)(2,1)}), bf16[16,16,416]{2,1,0:T(8,128)(2,1)S(1)}, u32[]{:S(2)}, u32[]{:S(2)}) %all-to-all-start.6) | async-done | bytes 213024 | tf_op jit(solution)/shard_map/all_to_all | solution.py:158
  160.1 1.1 shard_map.53
  161.3 0.2 reshape.19
  161.5 23.7 %all_to_all.45 = bf16[64,4,1024]{2,1,0:T(4,128)(2,1)S(1)} all-to-all(bf16[64,4,1024]{2,1,0:T(4,128)(2,1)S(1)} %reshape.19), channel_id=1, replica_groups=mesh['hid'=64,'z'=8,'core'=2] {'hid'}, dimensions={0} | all-to-all | bytes 1048576 | tf_op jit(solution)/shard_map/all_to_all | solution.py:158
  185.2 0.8 reduce_sum.12
  (1 shorter events, 0.0 us)
Async XLA Ops:
  0.0 0.7 copy-start.5
  0.7 25.0 %copy-start = (bf16[416,1024]{1,0:T(8,128)(2,1)S(1)}, bf16[416,1024]{1,0:T(8,128)(2,1)}, u32[]{:S(2)}) copy-start(bf16[416,1024]{1,0:T(8,128)(2,1)} %down.3) | copy-start | bytes 2555908
  1.5 38.9 %all-to-all-start = ((bf16[128,8,256]{2,1,0:T(8,128)(2,1)}), bf16[128,8,256]{2,1,0:T(8,128)(2,1)S(1)}, u32[]{:S(2)}, u32[]{:S(2)}) async-start(bf16[128,8,256]{2,1,0:T(8,128)(2,1)} %bitcast.5), calls=%async_computation | async-start | bytes 1048576 | tf_op jit(solution)/shard_map/all_to_all | solution.py:158
  20.9 7.4 %collective-permute-start = (bf16[416,1024]{1,0:T(8,128)(2,1)}, bf16[416,1024]{1,0:T(8,128)(2,1)S(1)}, u32[]{:S(2)}, u32[]{:S(2)}) collective-permute-start(bf16[416,1024]{1,0:T(8,128)(2,1)} %bitcast.11), channel_id=1, source_target_pairs={{0,1},{1,0},{2,3},{3,2},{4,5},{5,4},{6,7},{7,6},{8,9},{9,8},{10,11... | collective-permute-start | bytes 2555912 | tf_op jit(solution)/shard_map/ppermute | solution.py:175
  23.8 4.5 %collective-permute-start.1 = (bf16[416,1024]{1,0:T(8,128)(2,1)}, bf16[416,1024]{1,0:T(8,128)(2,1)S(1)}, u32[]{:S(2)}, u32[]{:S(2)}) collective-permute-start(bf16[416,1024]{1,0:T(8,128)(2,1)} %bitcast.14), channel_id=1, source_target_pairs={{0,1},{1,0},{2,3},{3,2},{4,5},{5,4},{6,7},{7,6},{8,9},{9,8},{10,11... | collective-permute-start | bytes 2555912 | tf_op jit(solution)/shard_map/ppermute | solution.py:175
  25.7 18.9 %collective-permute-start.2 = (bf16[416,1024]{1,0:T(8,128)(2,1)S(1)}, bf16[416,1024]{1,0:T(8,128)(2,1)}, u32[]{:S(2)}, u32[]{:S(2)}) collective-permute-start(bf16[416,1024]{1,0:T(8,128)(2,1)S(1)} %copy-done), channel_id=1, source_target_pairs={{0,1},{1,0},{2,3},{3,2},{4,5},{5,4},{6,7},{7,6},{8,9},{9,8},{10,11... | collective-permute-start | bytes 2555912 | tf_op jit(solution)/shard_map/ppermute | solution.py:176
  40.4 1.2 copy-start.1
  41.6 1.2 copy-start.3
  78.2 46.4 %copy-start.4 = (bf16[1024,416]{0,1:T(8,128)(2,1)S(1)}, bf16[1024,416]{0,1:T(8,128)(2,1)}, u32[]{:S(2)}) copy-start(bf16[1024,416]{0,1:T(8,128)(2,1)} %param.6) | copy-start | bytes 2555908
  101.6 23.0 %copy-start.2 = (bf16[1024,416]{0,1:T(8,128)(2,1)S(1)}, bf16[1024,416]{0,1:T(8,128)(2,1)}, u32[]{:S(2)}) copy-start(bf16[1024,416]{0,1:T(8,128)(2,1)} %param.5) | copy-start | bytes 2555908
  139.0 21.2 %all-to-all-start.6 = ((bf16[16,16,416]{2,1,0:T(8,128)(2,1)}), bf16[16,16,416]{2,1,0:T(8,128)(2,1)S(1)}, u32[]{:S(2)}, u32[]{:S(2)}) async-start(bf16[16,16,416]{2,1,0:T(8,128)(2,1)} %shard_map.52), calls=%async_computation.6 | async-start | bytes 524288 | tf_op jit(solution)/shard_map/all_to_all | solution.py:158
  148.3 3.1 %collective-permute-start.3 = (bf16[16,256]{1,0:T(8,128)(2,1)S(1)}, bf16[16,256]{1,0:T(8,128)(2,1)S(1)}, u32[]{:S(2)}, u32[]{:S(2)}) collective-permute-start(bf16[16,256]{1,0:T(8,128)(2,1)S(1)} %get-tuple-element.16), channel_id=1, source_target_pairs={{0,1},{1,0},{2,3},{3,2},{4,5},{5,4},{6,7},{7,6},{8,9},{9,8},{10,11... | collective-permute-start | bytes 24584 | tf_op jit(solution)/shard_map/ppermute | solution.py:218

commit v5 on v4

--- a/solution.py
+++ b/solution.py
@@ -11,7 +11,8 @@
 CORES = 2
 BLOCKS = 8
 F32, BF16 = jnp.float32, jnp.bfloat16
-VMEM_BYTES = 16 * 2**20
+VMEM_BYTES = 8 * 2**20
+FIRST_VMEM_BYTES = 60 * 2**20
 
 
 def dot(a, b):
@@ -22,9 +23,9 @@
     return lax.dot_general(a, b, (((1,), (1,)), ((), ())), preferred_element_type=F32)
 
 
-def kernel_call(body, out_shape, n_in, scalars=False, scratch=()):
+def kernel_call(body, out_shape, n_in, scalars=0, far=0, scratch=(), limit=VMEM_BYTES):
     vmem = pl.BlockSpec(memory_space=pltpu.VMEM)
-    specs = [pl.BlockSpec(memory_space=pltpu.SMEM)] if scalars else []
+    specs = [pl.BlockSpec(memory_space=pltpu.SMEM)] * scalars + [pl.BlockSpec(memory_space=pl.ANY)] * far
     single = not isinstance(out_shape, (list, tuple))
     return pl.pallas_call(
         body,
@@ -32,7 +33,7 @@
         in_specs=specs + [vmem] * n_in,
         out_specs=vmem if single else [vmem] * len(out_shape),
         scratch_shapes=scratch,
-        compiler_params=pltpu.CompilerParams(vmem_limit_bytes=VMEM_BYTES),
+        compiler_params=pltpu.CompilerParams(vmem_limit_bytes=limit),
     )
 
 
@@ -59,7 +60,21 @@
             out[h, c] = block
 
 
-def first_products(place, gathered, gate, up, gate_there, up_there, out, block, stream):
+def first_products(
+    place, gathered_far, gate_far, up_far, gate_there_far, up_there_far, out, block,
+    stream, gathered, gate, up, gate_there, up_there, sems,
+):
+    pairs = (
+        (gathered_far, gathered),
+        (gate_there_far, gate_there),
+        (up_there_far, up_there),
+        (gate_far, gate),
+        (up_far, up),
+    )
+    fetches = [pltpu.make_async_copy(*pair, sems.at[i]) for i, pair in enumerate(pairs)]
+    for fetch in fetches:
+        fetch.start()
+    fetches[0].wait()
     n_hid, cores, lines, cols = gathered.shape
     n_blocks, rows, _ = stream.shape
     half, parts = rows // n_hid, n_blocks // cores
@@ -82,20 +97,23 @@
         jnp.concatenate([stream[which * parts + k] for k in range(parts)], axis=1)
         for which in range(cores)
     )
-    store_partial(
-        out,
-        dot_t(x, gate[...]) + dot_t(y, gate_there[...]),
-        dot_t(x, up[...]) + dot_t(y, up_there[...]),
-    )
+    fetches[1].wait()
+    gate_sum = dot_t(y, gate_there[...])
+    fetches[2].wait()
+    up_sum = dot_t(y, up_there[...])
+    fetches[3].wait()
+    gate_sum += dot_t(x, gate[...])
+    fetches[4].wait()
+    up_sum += dot_t(x, up[...])
+    store_partial(out, gate_sum, up_sum)
 
 
 def block_products(blocks, gate, up, gate_there, up_there, out):
     n_rows, n_cols, rows, cols = blocks.shape
-    x = jnp.concatenate(
-        [blocks[:, k].reshape(n_rows * rows, cols) for k in range(n_cols)], axis=1
-    )
-    span = n_cols // 2 * cols
-    x, y = x[:, :span], x[:, span:]
+    x, y = (
+        jnp.concatenate([blocks[:, k].reshape(n_rows * rows, cols) for k in part], axis=1)
+        for part in (range(n_cols // 2), range(n_cols // 2, n_cols))
+    )
     store_partial(
         out,
         dot_t(x, gate[...]) + dot_t(y, gate_there[...]),
@@ -114,10 +132,14 @@
         out[k] = hidden
 
 
-def down_blocks(hidden, down, down_there, out):
+def down_blocks(there_far, hidden, down, out, down_there, sems):
+    fetch = pltpu.make_async_copy(there_far, down_there, sems.at[0])
+    fetch.start()
     n_rows, n_cols, rows, cols = out.shape
     x = hidden[...].reshape(n_rows * rows, hidden.shape[-1])
     for half, weight in enumerate((down, down_there)):
+        if half == 1:
+            fetch.wait()
         for k in range(n_cols // 2):
             value = dot(x, weight[:, k * cols : (k + 1) * cols])
             out[:, half * (n_cols // 2) + k] = value.astype(BF16).reshape(n_rows, rows, cols)
@@ -148,10 +170,27 @@
     x = dot(order.astype(F32).astype(BF16), hidden[...].reshape(total, units)).astype(BF16)
     own_rows = source(rows) == lax.broadcasted_iota(jnp.int32, (total, rows), 1) + place[0] * rows
     addend = dot(own_rows.astype(F32).astype(BF16), block[...])
-    for k in range(out.shape[1] // cols):
+    n_blocks, own = down.shape[1] // cols, out.shape[2] // (down.shape[1] // cols)
+    values, rolled = [], []
+    for k in range(n_blocks):
         value = dot(x, down[:, k * cols : (k + 1) * cols])
         value += jnp.where(place[1] == k, addend, 0.0)
-        out[:, k * cols : (k + 1) * cols] = value.astype(BF16)
+        values.append(value.reshape(total // (2 * own), 2 * own, cols))
+        rolled.append(pltpu.roll(values[-1], own, 1))
+    upper = lax.broadcasted_iota(jnp.int32, values[0].shape, 1) < own
+    for k in range(0, n_blocks, 2):
+        lines = slice(k * own, (k + 2) * own)
+        out[:, 0, lines] = jnp.where(upper, values[k], rolled[k + 1]).astype(BF16)
+        out[:, 1, lines] = jnp.where(upper, rolled[k], values[k + 1]).astype(BF16)
+
+
+def final_sum(parts, out):
+    total = parts[0].astype(F32)
+    for k in range(1, parts.shape[0]):
+        total += parts[k].astype(F32)
+    own, cols = out.shape[0], total.shape[1]
+    for k in range(out.shape[1] // cols):
+        out[:, k * cols : (k + 1) * cols] = total[k * own : (k + 1) * own].astype(BF16)
 
 
 def exchange(parts, axes):
@@ -183,9 +222,16 @@
     partial_value, block = kernel_call(
         first_products,
         [partial_shape, jax.ShapeDtypeStruct((block_rows, block_cols), BF16)],
-        5,
-        True,
-        [pltpu.VMEM((BLOCKS, rows, block_cols), BF16)],
+        0,
+        scalars=1,
+        far=5,
+        scratch=[
+            pltpu.VMEM((BLOCKS, rows, block_cols), BF16),
+            pltpu.VMEM(copies_shape.shape, BF16),
+            *(pltpu.VMEM(gate.shape, BF16) for _ in weights),
+            pltpu.SemaphoreType.DMA((5,)),
+        ],
+        limit=FIRST_VMEM_BYTES,
     )(
         jnp.stack([core, row_block, col_block]).astype(jnp.int32),
         gathered.reshape(copies_shape.shape),
@@ -202,7 +248,13 @@
         if last:
             break
         blocks_shape = jax.ShapeDtypeStruct((BLOCKS, BLOCKS, block_rows, block_cols), BF16)
-        down_part = kernel_call(down_blocks, blocks_shape, 3)(hidden, down, down_there)
+        down_part = kernel_call(
+            down_blocks,
+            blocks_shape,
+            2,
+            far=1,
+            scratch=[pltpu.VMEM(down.shape, BF16), pltpu.SemaphoreType.DMA((1,))],
+        )(down_there, hidden, down)
         parts = exchange(down_part.reshape(n_hid, block_rows, block_cols), "hid")
         block, copies = kernel_call(
             add_branch,
@@ -218,11 +270,11 @@
     block = jnp.where(in_own, block, swap(block))
     block_core = jnp.where(in_own, core, 1 - core)
     place = jnp.stack([row_block * CORES + block_core, col_block % (BLOCKS // 2)]).astype(jnp.int32)
-    branch = kernel_call(last_down, jax.ShapeDtypeStruct((CORES * rows, span), BF16), 3, True)(
-        place, hidden, down, block
-    )
-    parts = exchange(branch.reshape(n_hid, own, span), "hid")
-    return jnp.sum(parts.astype(F32), axis=0).astype(BF16)
+    n_lines = own * span // block_cols
+    branch_shape = jax.ShapeDtypeStruct((n_hid // 2, 2, n_lines, block_cols), BF16)
+    branch = kernel_call(last_down, branch_shape, 3, scalars=1)(place, hidden, down, block)
+    parts = exchange(branch.reshape(n_hid, n_lines, block_cols), "hid")
+    return kernel_call(final_sum, jax.ShapeDtypeStruct((own, span), BF16), 1)(parts)
 
 
 def solution(mesh):

time: 187 us -> 187 us (level)
  Pallas kernels: 7.47 us -> 10.2 us
  local copies, waits for them, and re-layouts: 3.22 us -> 0.73 us
    pallas_call x1, Pallas kernels: 1.85 us -> 4.7 us  [per_device(): kernel_call(first_products, [partial_shape, jax.ShapeDtypeStruct((block_r...]
    unnamed x12 -> x18, local copies, waits for them, and re-layouts: 3.02 us -> 0.73 us
  transfers between devices with their start and end apart: 6 -> 6, of which waited for: 3 -> 3; matrix products, arithmetic and copies ran while one was open for 0% -> 0% of each run, Pallas kernels for 1% -> 3%
where the time goes in v5:
time: 187 us; the launch traced here: 186 us
  blocking collectives  114 us (61%)
  starting transfers between devices  39 us (21%)
  waiting for transfers between devices  20.8 us (11%)
  Pallas kernels  10.2 us (5%)
    all_to_all x6, blocking collectives, exchange(): return lax.all_to_all(parts, axes, 0, 0, tiled=True)  114 us
    all_to_all x2, starting transfers between devices, exchange(): return lax.all_to_all(parts, axes, 0, 0, tiled=True)  29.5 us
    all_to_all x2, waiting for transfers between devices, exchange(): return lax.all_to_all(parts, axes, 0, 0, tiled=True)  20 us
    ppermute x2, starting transfers between devices, per_device(): weights = (gate, up, swap(gate), swap(up))  4.91 us
    pallas_call x1, Pallas kernels, per_device(): kernel_call(first_products, [partial_shape, jax.ShapeDtypeStruct((block_r...  4.7 us
  transfers between devices with their start and end apart: 6, of which 3 were waited for; matrix products, arithmetic and copies ran while one was open for 0% of the time, Pallas kernels for 3%

profile of v5, /device:TPU:1, one launch (start us, length us, event | category | flops | bytes accessed | tf_op | source)
XLA Modules:
  0.0 185.8 jit_solution(1548195318571291384)
XLA Ops:
  0.0 0.0 copy-start.7
  0.0 0.7 copy-done.7
  0.7 0.0 copy-start
  0.7 0.8 shard_map.46
  1.5 20.4 %all-to-all-start = ((bf16[128,8,256]{2,1,0:T(8,128)(2,1)}), bf16[128,8,256]{2,1,0:T(8,128)(2,1)}, u32[]{:S(2)}, u32[]{:S(2)}) async-start(bf16[128,8,256]{2,1,0:T(8,128)(2,1)} %bitcast.5), calls=%async_computation | async-start | bytes 1048576 | tf_op jit(solution)/shard_map/all_to_all | solution.py:197
  21.9 3.0 %collective-permute-start = (bf16[416,1024]{1,0:T(8,128)(2,1)}, bf16[416,1024]{1,0:T(8,128)(2,1)S(1)}, u32[]{:S(2)}, u32[]{:S(2)}) collective-permute-start(bf16[416,1024]{1,0:T(8,128)(2,1)} %bitcast.12), channel_id=1, source_target_pairs={{0,1},{1,0},{2,3},{3,2},{4,5},{5,4},{6,7},{7,6},{8,9},{9,8},{10,11... | collective-permute-start | bytes 2555912 | tf_op jit(solution)/shard_map/ppermute | solution.py:214
  24.9 1.9 %collective-permute-start.1 = (bf16[416,1024]{1,0:T(8,128)(2,1)}, bf16[416,1024]{1,0:T(8,128)(2,1)S(1)}, u32[]{:S(2)}, u32[]{:S(2)}) collective-permute-start(bf16[416,1024]{1,0:T(8,128)(2,1)} %bitcast.15), channel_id=1, source_target_pairs={{0,1},{1,0},{2,3},{3,2},{4,5},{5,4},{6,7},{7,6},{8,9},{9,8},{10,11... | collective-permute-start | bytes 2555912 | tf_op jit(solution)/shard_map/ppermute | solution.py:214
  26.8 0.0 copy-done
  26.9 2.4 %collective-permute-start.2 = (bf16[416,1024]{1,0:T(8,128)(2,1)S(1)}, bf16[416,1024]{1,0:T(8,128)(2,1)S(1)}, u32[]{:S(2)}, u32[]{:S(2)}) collective-permute-start(bf16[416,1024]{1,0:T(8,128)(2,1)S(1)} %copy-done), channel_id=1, source_target_pairs={{0,1},{1,0},{2,3},{3,2},{4,5},{5,4},{6,7},{7,6},{8,9},{9,8},{10,11... | collective-permute-start | bytes 2555912 | tf_op jit(solution)/shard_map/ppermute | solution.py:215
  29.3 0.7 pad_add_fusion.1.place
  30.0 0.0 collective-permute-done.gate_there_far.gate_there
  30.0 0.0 copy-start.3
  30.0 0.0 collective-permute-done.1.up_there_far.up_there
  30.0 0.0 copy-start.5
  30.0 11.2 %all-to-all-done = bf16[128,8,256]{2,1,0:T(8,128)(2,1)} async-done(((bf16[128,8,256]{2,1,0:T(8,128)(2,1)}), bf16[128,8,256]{2,1,0:T(8,128)(2,1)}, u32[]{:S(2)}, u32[]{:S(2)}) %all-to-all-start) | async-done | bytes 524320 | tf_op jit(solution)/shard_map/all_to_all | solution.py:197
  41.1 0.0 copy-done.3
  41.1 0.0 copy-done.5
  41.1 4.7 %shard_map.47 = (bf16[8,32,416]{2,1,0:T(8,128)(2,1)}, bf16[16,256]{1,0:T(8,128)(2,1)}) custom-call(s32[3]{0:T(128)} %pad_add_fusion.1.place, bf16[64,2,8,256]{3,2,1,0:T(8,128)(2,1)} %bitcast.6.gathered_far, bf16[416,1024]{1,0:T(8,128)(2,1)} %bitcast.13, bf16[416,1024]{1,0:T(8,128)(2,1)} %bitcast.16, bf16[416,1024]{1,0:T(8,128)(2,1)} %copy-done.3, ...), custom_call_target="tpu_custom_call" | custom-call | tf_op jit(solution)/shard_map/pallas_call | solution.py:222
  45.8 0.0 collective-permute-done.2.there_far
  45.9 21.2 %all_to_all.40.parts = bf16[8,32,416]{2,1,0:T(8,128)(2,1)S(1)} all-to-all(bf16[8,32,416]{2,1,0:T(8,128)(2,1)} %get-tuple-element.13), channel_id=1, replica_groups=mesh['hid'=64,'z'=8,'core'=2] {'z'}, dimensions={0} | all-to-all | bytes 425984 | tf_op jit(solution)/shard_map/all_to_all | solution.py:197
  67.0 0.1 shard_map.48
  67.1 10.4 %all_to_all.41.hidden = bf16[8,16,416]{2,1,0:T(8,128)(2,1)S(1)} all-to-all(bf16[8,16,416]{2,1,0:T(8,128)(2,1)S(1)} %shard_map.48), channel_id=1, replica_groups=mesh['hid'=64,'z'=8,'core'=2] {'z'}, dimensions={0} | all-to-all | bytes 212992 | tf_op jit(solution)/shard_map/all_to_all | solution.py:197
  77.5 0.0 copy-start.8
  77.5 0.0 copy-start.6
  77.5 0.8 shard_map.49
  78.3 0.0 copy-start.2
  78.3 0.0 copy-start.4
  78.3 23.3 %all_to_all.42.parts = bf16[64,16,256]{2,1,0:T(8,128)(2,1)S(1)} all-to-all(bf16[64,16,256]{2,1,0:T(8,128)(2,1)S(1)} %bitcast.19), channel_id=1, replica_groups=mesh['hid'=64,'z'=8,'core'=2] {'hid'}, dimensions={0} | all-to-all | bytes 1048576 | tf_op jit(solution)/shard_map/all_to_all | solution.py:197
  101.6 0.0 copy-start.1
  101.6 0.0 copy-done.8
  101.6 0.1 shard_map.50
  101.7 22.9 %all_to_all.43 = bf16[64,16,256]{2,1,0:T(8,128)(2,1)S(1)} all-to-all(bf16[64,16,256]{2,1,0:T(8,128)(2,1)S(1)} %get-tuple-element.15), channel_id=1, replica_groups=mesh['hid'=64,'z'=8,'core'=2] {'hid'}, dimensions={0} | all-to-all | bytes 1048576 | tf_op jit(solution)/shard_map/all_to_all | solution.py:197
  124.6 0.0 copy-done.6
  124.6 0.0 copy-done.2
  124.6 0.0 copy-done.4
  124.6 0.0 copy-done.1
  124.6 1.1 shard_map.51
  125.8 12.6 %all_to_all.44.parts = bf16[8,32,416]{2,1,0:T(8,128)(2,1)S(1)} all-to-all(bf16[8,32,416]{2,1,0:T(8,128)(2,1)S(1)} %shard_map.51), channel_id=1, replica_groups=mesh['hid'=64,'z'=8,'core'=2] {'z'}, dimensions={0} | all-to-all | bytes 425984 | tf_op jit(solution)/shard_map/all_to_all | solution.py:197
  138.4 0.8 shard_map.52
  139.2 9.2 %all-to-all-start.6 = ((bf16[16,16,416]{2,1,0:T(8,128)(2,1)}), bf16[16,16,416]{2,1,0:T(8,128)(2,1)S(1)}, u32[]{:S(2)}, u32[]{:S(2)}) async-start(bf16[16,16,416]{2,1,0:T(8,128)(2,1)} %shard_map.52), calls=%async_computation.6 | async-start | bytes 524288 | tf_op jit(solution)/shard_map/all_to_all | solution.py:197
  148.4 2.2 %collective-permute-start.3 = (bf16[16,256]{1,0:T(8,128)(2,1)S(1)}, bf16[16,256]{1,0:T(8,128)(2,1)S(1)}, u32[]{:S(2)}, u32[]{:S(2)}) collective-permute-start(bf16[16,256]{1,0:T(8,128)(2,1)S(1)} %get-tuple-element.16), channel_id=1, source_target_pairs={{0,1},{1,0},{2,3},{3,2},{4,5},{5,4},{6,7},{7,6},{8,9},{9,8},{10,11... | collective-permute-start | bytes 24584 | tf_op jit(solution)/shard_map/ppermute | solution.py:270
  150.5 0.1 pad_add_fusion.place
  150.6 0.8 collective-permute-done.3
  151.4 8.8 %all-to-all-done.6.hidden = bf16[16,16,416]{2,1,0:T(8,128)(2,1)S(1)} async-done(((bf16[16,16,416]{2,1,0:T(8,128)(2,1)}), bf16[16,16,416]{2,1,0:T(8,128)(2,1)S(1)}, u32[]{:S(2)}, u32[]{:S(2)}) %all-to-all-start.6) | async-done | bytes 213024 | tf_op jit(solution)/shard_map/all_to_all | solution.py:197
  160.2 1.1 shard_map.53
  161.4 23.7 %all_to_all.45.parts = bf16[64,16,256]{2,1,0:T(8,128)(2,1)S(1)} all-to-all(bf16[64,16,256]{2,1,0:T(8,128)(2,1)S(1)} %bitcast.18), channel_id=1, replica_groups=mesh['hid'=64,'z'=8,'core'=2] {'hid'}, dimensions={0} | all-to-all | bytes 1048576 | tf_op jit(solution)/shard_map/all_to_all | solution.py:197
  185.1 0.7 shard_map.54
  (1 shorter events, 0.0 us)
Async XLA Ops:
  0.0 0.7 copy-start.7
  0.7 26.1 %copy-start = (bf16[416,1024]{1,0:T(8,128)(2,1)S(1)}, bf16[416,1024]{1,0:T(8,128)(2,1)}, u32[]{:S(2)}) copy-start(bf16[416,1024]{1,0:T(8,128)(2,1)} %down.3) | copy-start | bytes 2555908
  1.5 39.6 %all-to-all-start = ((bf16[128,8,256]{2,1,0:T(8,128)(2,1)}), bf16[128,8,256]{2,1,0:T(8,128)(2,1)}, u32[]{:S(2)}, u32[]{:S(2)}) async-start(bf16[128,8,256]{2,1,0:T(8,128)(2,1)} %bitcast.5), calls=%async_computation | async-start | bytes 1048576 | tf_op jit(solution)/shard_map/all_to_all | solution.py:197
  21.9 8.0 %collective-permute-start = (bf16[416,1024]{1,0:T(8,128)(2,1)}, bf16[416,1024]{1,0:T(8,128)(2,1)S(1)}, u32[]{:S(2)}, u32[]{:S(2)}) collective-permute-start(bf16[416,1024]{1,0:T(8,128)(2,1)} %bitcast.12), channel_id=1, source_target_pairs={{0,1},{1,0},{2,3},{3,2},{4,5},{5,4},{6,7},{7,6},{8,9},{9,8},{10,11... | collective-permute-start | bytes 2555912 | tf_op jit(solution)/shard_map/ppermute | solution.py:214
  24.9 5.1 %collective-permute-start.1 = (bf16[416,1024]{1,0:T(8,128)(2,1)}, bf16[416,1024]{1,0:T(8,128)(2,1)S(1)}, u32[]{:S(2)}, u32[]{:S(2)}) collective-permute-start(bf16[416,1024]{1,0:T(8,128)(2,1)} %bitcast.15), channel_id=1, source_target_pairs={{0,1},{1,0},{2,3},{3,2},{4,5},{5,4},{6,7},{7,6},{8,9},{9,8},{10,11... | collective-permute-start | bytes 2555912 | tf_op jit(solution)/shard_map/ppermute | solution.py:214
  26.9 19.0 %collective-permute-start.2 = (bf16[416,1024]{1,0:T(8,128)(2,1)S(1)}, bf16[416,1024]{1,0:T(8,128)(2,1)S(1)}, u32[]{:S(2)}, u32[]{:S(2)}) collective-permute-start(bf16[416,1024]{1,0:T(8,128)(2,1)S(1)} %copy-done), channel_id=1, source_target_pairs={{0,1},{1,0},{2,3},{3,2},{4,5},{5,4},{6,7},{7,6},{8,9},{9,8},{10,11... | collective-permute-start | bytes 2555912 | tf_op jit(solution)/shard_map/ppermute | solution.py:215
  30.0 11.2 %copy-start.3 = (bf16[416,1024]{1,0:T(8,128)(2,1)}, bf16[416,1024]{1,0:T(8,128)(2,1)S(1)}, u32[]{:S(2)}) copy-start(bf16[416,1024]{1,0:T(8,128)(2,1)S(1)} %collective-permute-done.gate_there_far.gate_there) | copy-start | bytes 2555908
  30.0 11.2 %copy-start.5 = (bf16[416,1024]{1,0:T(8,128)(2,1)}, bf16[416,1024]{1,0:T(8,128)(2,1)S(1)}, u32[]{:S(2)}) copy-start(bf16[416,1024]{1,0:T(8,128)(2,1)S(1)} %collective-permute-done.1.up_there_far.up_there) | copy-start | bytes 2555908
  77.5 24.1 %copy-start.8 = (bf16[16,256]{1,0:T(8,128)(2,1)S(1)}, bf16[16,256]{1,0:T(8,128)(2,1)}, u32[]{:S(2)}) copy-start(bf16[16,256]{1,0:T(8,128)(2,1)} %get-tuple-element.14.block) | copy-start | bytes 24580
  77.5 47.1 %copy-start.6 = (bf16[416,1024]{1,0:T(8,128)(2,1)S(1)}, bf16[416,1024]{1,0:T(8,128)(2,1)}, u32[]{:S(2)}) copy-start(bf16[416,1024]{1,0:T(8,128)(2,1)} %copy-done.5) | copy-start | bytes 2555908
  78.3 46.4 %copy-start.2 = (bf16[1024,416]{0,1:T(8,128)(2,1)S(1)}, bf16[1024,416]{0,1:T(8,128)(2,1)}, u32[]{:S(2)}) copy-start(bf16[1024,416]{0,1:T(8,128)(2,1)} %param.6) | copy-start | bytes 2555908
  78.3 46.4 %copy-start.4 = (bf16[416,1024]{1,0:T(8,128)(2,1)S(1)}, bf16[416,1024]{1,0:T(8,128)(2,1)}, u32[]{:S(2)}) copy-start(bf16[416,1024]{1,0:T(8,128)(2,1)} %copy-done.3) | copy-start | bytes 2555908
  101.6 23.1 %copy-start.1 = (bf16[1024,416]{0,1:T(8,128)(2,1)S(1)}, bf16[1024,416]{0,1:T(8,128)(2,1)}, u32[]{:S(2)}) copy-start(bf16[1024,416]{0,1:T(8,128)(2,1)} %param.5) | copy-start | bytes 2555908
  139.2 21.0 %all-to-all-start.6 = ((bf16[16,16,416]{2,1,0:T(8,128)(2,1)}), bf16[16,16,416]{2,1,0:T(8,128)(2,1)S(1)}, u32[]{:S(2)}, u32[]{:S(2)}) async-start(bf16[16,16,416]{2,1,0:T(8,128)(2,1)} %shard_map.52), calls=%async_computation.6 | async-start | bytes 524288 | tf_op jit(solution)/shard_map/all_to_all | solution.py:197
  148.4 3.1 %collective-permute-start.3 = (bf16[16,256]{1,0:T(8,128)(2,1)S(1)}, bf16[16,256]{1,0:T(8,128)(2,1)S(1)}, u32[]{:S(2)}, u32[]{:S(2)}) collective-permute-start(bf16[16,256]{1,0:T(8,128)(2,1)S(1)} %get-tuple-element.16), channel_id=1, source_target_pairs={{0,1},{1,0},{2,3},{3,2},{4,5},{5,4},{6,7},{7,6},{8,9},{9,8},{10,11... | collective-permute-start | bytes 24584 | tf_op jit(solution)/shard_map/ppermute | solution.py:270

commit v6 on v5

--- a/solution.py
+++ b/solution.py
@@ -8,11 +8,12 @@
 from jax.sharding import Mesh, PartitionSpec as P
 
 STEPS = 2
+FETCHES = 2
 CORES = 2
 BLOCKS = 8
 F32, BF16 = jnp.float32, jnp.bfloat16
 VMEM_BYTES = 8 * 2**20
-FIRST_VMEM_BYTES = 60 * 2**20
+FIRST_VMEM_BYTES = 53 * 2**20
 
 
 def dot(a, b):
@@ -61,20 +62,33 @@
 
 
 def first_products(
-    place, gathered_far, gate_far, up_far, gate_there_far, up_there_far, out, block,
-    stream, gathered, gate, up, gate_there, up_there, sems,
+    place, gate_far, up_far, gate_there_far, up_there_far, gathered, out, block,
+    stream, gate, up, gate_there, up_there, sems,
 ):
     pairs = (
-        (gathered_far, gathered),
         (gate_there_far, gate_there),
         (up_there_far, up_there),
         (gate_far, gate),
         (up_far, up),
     )
-    fetches = [pltpu.make_async_copy(*pair, sems.at[i]) for i, pair in enumerate(pairs)]
-    for fetch in fetches:
-        fetch.start()
-    fetches[0].wait()
+    part = gate.shape[0] // FETCHES
+    fetches = [
+        [
+            pltpu.make_async_copy(
+                far.at[pl.ds(k * part, part)], near.at[pl.ds(k * part, part)], sems.at[i, k]
+            )
+            for k in range(FETCHES)
+        ]
+        for i, (far, near) in enumerate(pairs)
+    ]
+    for group in fetches:
+        for fetch in group:
+            fetch.start()
+
+    def arrive(i):
+        for fetch in fetches[i]:
+            fetch.wait()
+
     n_hid, cores, lines, cols = gathered.shape
     n_blocks, rows, _ = stream.shape
     half, parts = rows // n_hid, n_blocks // cores
@@ -97,13 +111,13 @@
         jnp.concatenate([stream[which * parts + k] for k in range(parts)], axis=1)
         for which in range(cores)
     )
-    fetches[1].wait()
+    arrive(0)
     gate_sum = dot_t(y, gate_there[...])
-    fetches[2].wait()
+    arrive(1)
     up_sum = dot_t(y, up_there[...])
-    fetches[3].wait()
+    arrive(2)
     gate_sum += dot_t(x, gate[...])
-    fetches[4].wait()
+    arrive(3)
     up_sum += dot_t(x, up[...])
     store_partial(out, gate_sum, up_sum)
 
@@ -222,20 +236,19 @@
     partial_value, block = kernel_call(
         first_products,
         [partial_shape, jax.ShapeDtypeStruct((block_rows, block_cols), BF16)],
-        0,
+        1,
         scalars=1,
-        far=5,
+        far=4,
         scratch=[
             pltpu.VMEM((BLOCKS, rows, block_cols), BF16),
-            pltpu.VMEM(copies_shape.shape, BF16),
             *(pltpu.VMEM(gate.shape, BF16) for _ in weights),
-            pltpu.SemaphoreType.DMA((5,)),
+            pltpu.SemaphoreType.DMA((4, FETCHES)),
         ],
         limit=FIRST_VMEM_BYTES,
     )(
         jnp.stack([core, row_block, col_block]).astype(jnp.int32),
+        *weights,
         gathered.reshape(copies_shape.shape),
-        *weights,
     )
     partial_value, down_there = lax.optimization_barrier((partial_value, down_there))
     for repeat in range(STEPS):

time: 187 us -> 186 us (level)
  transfers between devices with their start and end apart: 6 -> 6, of which waited for: 3 -> 3; matrix products, arithmetic and copies ran while one was open for 0% -> 0% of each run, Pallas kernels for 3% -> 2%
where the time goes in v6:
time: 186 us; the launch traced here: 185 us
  blocking collectives  114 us (61%)
  starting transfers between devices  37.9 us (20%)
  waiting for transfers between devices  21.8 us (12%)
  Pallas kernels  10 us (5%)
    all_to_all x6, blocking collectives, exchange(): return lax.all_to_all(parts, axes, 0, 0, tiled=True)  114 us
    all_to_all x2, starting transfers between devices, exchange(): return lax.all_to_all(parts, axes, 0, 0, tiled=True)  28.5 us
    all_to_all x2, waiting for transfers between devices, exchange(): return lax.all_to_all(parts, axes, 0, 0, tiled=True)  21 us
    ppermute x2, starting transfers between devices, per_device(): weights = (gate, up, swap(gate), swap(up))  4.84 us
    pallas_call x1, Pallas kernels, per_device(): kernel_call(first_products, [partial_shape, jax.ShapeDtypeStruct((block_r...  3.74 us
  transfers between devices with their start and end apart: 6, of which 3 were waited for; matrix products, arithmetic and copies ran while one was open for 0% of the time, Pallas kernels for 2%

profile of v6, /device:TPU:1, one launch (start us, length us, event | category | flops | bytes accessed | tf_op | source)
XLA Modules:
  0.0 185.3 jit_solution(16867685621208799918)
XLA Ops:
  0.0 0.0 copy-start.7
  0.0 0.7 copy-done.7
  0.7 0.0 copy-start
  0.7 0.8 shard_map.46
  1.5 19.3 %all-to-all-start = ((bf16[128,8,256]{2,1,0:T(8,128)(2,1)}), bf16[128,8,256]{2,1,0:T(8,128)(2,1)S(1)}, u32[]{:S(2)}, u32[]{:S(2)}) async-start(bf16[128,8,256]{2,1,0:T(8,128)(2,1)} %bitcast.7), calls=%async_computation | async-start | bytes 1048576 | tf_op jit(solution)/shard_map/all_to_all | solution.py:211
  20.9 2.9 %collective-permute-start = (bf16[416,1024]{1,0:T(8,128)(2,1)}, bf16[416,1024]{1,0:T(8,128)(2,1)S(1)}, u32[]{:S(2)}, u32[]{:S(2)}) collective-permute-start(bf16[416,1024]{1,0:T(8,128)(2,1)} %bitcast.12), channel_id=1, source_target_pairs={{0,1},{1,0},{2,3},{3,2},{4,5},{5,4},{6,7},{7,6},{8,9},{9,8},{10,11... | collective-permute-start | bytes 2555912 | tf_op jit(solution)/shard_map/ppermute | solution.py:228
  23.8 1.9 %collective-permute-start.1 = (bf16[416,1024]{1,0:T(8,128)(2,1)}, bf16[416,1024]{1,0:T(8,128)(2,1)S(1)}, u32[]{:S(2)}, u32[]{:S(2)}) collective-permute-start(bf16[416,1024]{1,0:T(8,128)(2,1)} %bitcast.15), channel_id=1, source_target_pairs={{0,1},{1,0},{2,3},{3,2},{4,5},{5,4},{6,7},{7,6},{8,9},{9,8},{10,11... | collective-permute-start | bytes 2555912 | tf_op jit(solution)/shard_map/ppermute | solution.py:228
  25.7 0.0 copy-done
  25.7 2.4 %collective-permute-start.2 = (bf16[416,1024]{1,0:T(8,128)(2,1)S(1)}, bf16[416,1024]{1,0:T(8,128)(2,1)}, u32[]{:S(2)}, u32[]{:S(2)}) collective-permute-start(bf16[416,1024]{1,0:T(8,128)(2,1)S(1)} %copy-done), channel_id=1, source_target_pairs={{0,1},{1,0},{2,3},{3,2},{4,5},{5,4},{6,7},{7,6},{8,9},{9,8},{10,11... | collective-permute-start | bytes 2555912 | tf_op jit(solution)/shard_map/ppermute | solution.py:229
  28.2 0.1 pad_add_fusion.1.place
  28.2 0.0 collective-permute-done.gate_there_far.gate_there
  28.2 0.0 copy-start.3
  28.3 0.0 collective-permute-done.1.up_there_far.up_there
  28.3 0.0 copy-start.5
  28.3 12.2 %all-to-all-done = bf16[128,8,256]{2,1,0:T(8,128)(2,1)S(1)} async-done(((bf16[128,8,256]{2,1,0:T(8,128)(2,1)}), bf16[128,8,256]{2,1,0:T(8,128)(2,1)S(1)}, u32[]{:S(2)}, u32[]{:S(2)}) %all-to-all-start) | async-done | bytes 524320 | tf_op jit(solution)/shard_map/all_to_all | solution.py:211
  40.4 0.0 copy-done.3
  40.4 0.0 copy-done.5
  40.4 3.7 %shard_map.47 = (bf16[8,32,416]{2,1,0:T(8,128)(2,1)S(1)}, bf16[16,256]{1,0:T(8,128)(2,1)S(1)}) custom-call(s32[3]{0:T(128)S(1)} %pad_add_fusion.1.place, bf16[416,1024]{1,0:T(8,128)(2,1)} %bitcast.13, bf16[416,1024]{1,0:T(8,128)(2,1)} %bitcast.16, bf16[416,1024]{1,0:T(8,128)(2,1)} %copy-done.3, bf16[416,1024]{1,0:T(8,128)(2,1)} %copy-done.5, ...), custom_call_target="tpu_custom_call" | custom-call | tf_op jit(solution)/shard_map/pallas_call | solution.py:236
  44.2 0.0 collective-permute-done.2.there_far
  44.2 21.5 %all_to_all.40.parts = bf16[8,32,416]{2,1,0:T(8,128)(2,1)S(1)} all-to-all(bf16[8,32,416]{2,1,0:T(8,128)(2,1)S(1)} %get-tuple-element.13), channel_id=1, replica_groups=mesh['hid'=64,'z'=8,'core'=2] {'z'}, dimensions={0} | all-to-all | bytes 425984 | tf_op jit(solution)/shard_map/all_to_all | solution.py:211
  65.7 0.1 shard_map.48
  65.8 10.4 %all_to_all.41.hidden = bf16[8,16,416]{2,1,0:T(8,128)(2,1)S(1)} all-to-all(bf16[8,16,416]{2,1,0:T(8,128)(2,1)S(1)} %shard_map.48), channel_id=1, replica_groups=mesh['hid'=64,'z'=8,'core'=2] {'z'}, dimensions={0} | all-to-all | bytes 212992 | tf_op jit(solution)/shard_map/all_to_all | solution.py:211
  76.2 0.0 copy-start.6
  76.2 1.6 shard_map.49
  77.8 0.0 copy-start.2
  77.8 0.0 copy-start.4
  77.8 23.3 %all_to_all.42.parts = bf16[64,16,256]{2,1,0:T(8,128)(2,1)S(1)} all-to-all(bf16[64,16,256]{2,1,0:T(8,128)(2,1)S(1)} %bitcast.20), channel_id=1, replica_groups=mesh['hid'=64,'z'=8,'core'=2] {'hid'}, dimensions={0} | all-to-all | bytes 1048576 | tf_op jit(solution)/shard_map/all_to_all | solution.py:211
  101.1 0.0 copy-start.1
  101.1 0.1 shard_map.50
  101.2 22.9 %all_to_all.43 = bf16[64,16,256]{2,1,0:T(8,128)(2,1)S(1)} all-to-all(bf16[64,16,256]{2,1,0:T(8,128)(2,1)S(1)} %get-tuple-element.15), channel_id=1, replica_groups=mesh['hid'=64,'z'=8,'core'=2] {'hid'}, dimensions={0} | all-to-all | bytes 1048576 | tf_op jit(solution)/shard_map/all_to_all | solution.py:211
  124.1 0.0 copy-done.6
  124.1 0.0 copy-done.2
  124.1 0.0 copy-done.4
  124.1 0.0 copy-done.1
  124.2 1.1 shard_map.51
  125.3 12.6 %all_to_all.44.parts = bf16[8,32,416]{2,1,0:T(8,128)(2,1)S(1)} all-to-all(bf16[8,32,416]{2,1,0:T(8,128)(2,1)S(1)} %shard_map.51), channel_id=1, replica_groups=mesh['hid'=64,'z'=8,'core'=2] {'z'}, dimensions={0} | all-to-all | bytes 425984 | tf_op jit(solution)/shard_map/all_to_all | solution.py:211
  137.9 0.8 shard_map.52
  138.6 9.2 %all-to-all-start.6 = ((bf16[16,16,416]{2,1,0:T(8,128)(2,1)}), bf16[16,16,416]{2,1,0:T(8,128)(2,1)S(1)}, u32[]{:S(2)}, u32[]{:S(2)}) async-start(bf16[16,16,416]{2,1,0:T(8,128)(2,1)} %shard_map.52), calls=%async_computation.6 | async-start | bytes 524288 | tf_op jit(solution)/shard_map/all_to_all | solution.py:211
  147.8 2.2 %collective-permute-start.3 = (bf16[16,256]{1,0:T(8,128)(2,1)S(1)}, bf16[16,256]{1,0:T(8,128)(2,1)S(1)}, u32[]{:S(2)}, u32[]{:S(2)}) collective-permute-start(bf16[16,256]{1,0:T(8,128)(2,1)S(1)} %get-tuple-element.16), channel_id=1, source_target_pairs={{0,1},{1,0},{2,3},{3,2},{4,5},{5,4},{6,7},{7,6},{8,9},{9,8},{10,11... | collective-permute-start | bytes 24584 | tf_op jit(solution)/shard_map/ppermute | solution.py:283
  150.0 0.1 pad_add_fusion.place
  150.1 0.8 collective-permute-done.3
  150.9 8.8 %all-to-all-done.6.hidden = bf16[16,16,416]{2,1,0:T(8,128)(2,1)S(1)} async-done(((bf16[16,16,416]{2,1,0:T(8,128)(2,1)}), bf16[16,16,416]{2,1,0:T(8,128)(2,1)S(1)}, u32[]{:S(2)}, u32[]{:S(2)}) %all-to-all-start.6) | async-done | bytes 213024 | tf_op jit(solution)/shard_map/all_to_all | solution.py:211
  159.7 1.1 shard_map.53
  160.8 23.7 %all_to_all.45.parts = bf16[64,16,256]{2,1,0:T(8,128)(2,1)S(1)} all-to-all(bf16[64,16,256]{2,1,0:T(8,128)(2,1)S(1)} %bitcast.19), channel_id=1, replica_groups=mesh['hid'=64,'z'=8,'core'=2] {'hid'}, dimensions={0} | all-to-all | bytes 1048576 | tf_op jit(solution)/shard_map/all_to_all | solution.py:211
  184.6 0.7 shard_map.54
  (1 shorter events, 0.0 us)
Async XLA Ops:
  0.0 0.7 copy-start.7
  0.7 25.0 %copy-start = (bf16[416,1024]{1,0:T(8,128)(2,1)S(1)}, bf16[416,1024]{1,0:T(8,128)(2,1)}, u32[]{:S(2)}) copy-start(bf16[416,1024]{1,0:T(8,128)(2,1)} %down.3) | copy-start | bytes 2555908
  1.5 38.9 %all-to-all-start = ((bf16[128,8,256]{2,1,0:T(8,128)(2,1)}), bf16[128,8,256]{2,1,0:T(8,128)(2,1)S(1)}, u32[]{:S(2)}, u32[]{:S(2)}) async-start(bf16[128,8,256]{2,1,0:T(8,128)(2,1)} %bitcast.7), calls=%async_computation | async-start | bytes 1048576 | tf_op jit(solution)/shard_map/all_to_all | solution.py:211
  20.9 7.4 %collective-permute-start = (bf16[416,1024]{1,0:T(8,128)(2,1)}, bf16[416,1024]{1,0:T(8,128)(2,1)S(1)}, u32[]{:S(2)}, u32[]{:S(2)}) collective-permute-start(bf16[416,1024]{1,0:T(8,128)(2,1)} %bitcast.12), channel_id=1, source_target_pairs={{0,1},{1,0},{2,3},{3,2},{4,5},{5,4},{6,7},{7,6},{8,9},{9,8},{10,11... | collective-permute-start | bytes 2555912 | tf_op jit(solution)/shard_map/ppermute | solution.py:228
  23.8 4.5 %collective-permute-start.1 = (bf16[416,1024]{1,0:T(8,128)(2,1)}, bf16[416,1024]{1,0:T(8,128)(2,1)S(1)}, u32[]{:S(2)}, u32[]{:S(2)}) collective-permute-start(bf16[416,1024]{1,0:T(8,128)(2,1)} %bitcast.15), channel_id=1, source_target_pairs={{0,1},{1,0},{2,3},{3,2},{4,5},{5,4},{6,7},{7,6},{8,9},{9,8},{10,11... | collective-permute-start | bytes 2555912 | tf_op jit(solution)/shard_map/ppermute | solution.py:228
  25.7 18.5 %collective-permute-start.2 = (bf16[416,1024]{1,0:T(8,128)(2,1)S(1)}, bf16[416,1024]{1,0:T(8,128)(2,1)}, u32[]{:S(2)}, u32[]{:S(2)}) collective-permute-start(bf16[416,1024]{1,0:T(8,128)(2,1)S(1)} %copy-done), channel_id=1, source_target_pairs={{0,1},{1,0},{2,3},{3,2},{4,5},{5,4},{6,7},{7,6},{8,9},{9,8},{10,11... | collective-permute-start | bytes 2555912 | tf_op jit(solution)/shard_map/ppermute | solution.py:229
  28.2 12.2 %copy-start.3 = (bf16[416,1024]{1,0:T(8,128)(2,1)}, bf16[416,1024]{1,0:T(8,128)(2,1)S(1)}, u32[]{:S(2)}) copy-start(bf16[416,1024]{1,0:T(8,128)(2,1)S(1)} %collective-permute-done.gate_there_far.gate_there) | copy-start | bytes 2555908
  28.3 12.2 %copy-start.5 = (bf16[416,1024]{1,0:T(8,128)(2,1)}, bf16[416,1024]{1,0:T(8,128)(2,1)S(1)}, u32[]{:S(2)}) copy-start(bf16[416,1024]{1,0:T(8,128)(2,1)S(1)} %collective-permute-done.1.up_there_far.up_there) | copy-start | bytes 2555908
  76.2 47.9 %copy-start.6 = (bf16[416,1024]{1,0:T(8,128)(2,1)S(1)}, bf16[416,1024]{1,0:T(8,128)(2,1)}, u32[]{:S(2)}) copy-start(bf16[416,1024]{1,0:T(8,128)(2,1)} %copy-done.5) | copy-start | bytes 2555908
  77.8 46.4 %copy-start.2 = (bf16[1024,416]{0,1:T(8,128)(2,1)S(1)}, bf16[1024,416]{0,1:T(8,128)(2,1)}, u32[]{:S(2)}) copy-start(bf16[1024,416]{0,1:T(8,128)(2,1)} %param.6) | copy-start | bytes 2555908
  77.8 46.4 %copy-start.4 = (bf16[416,1024]{1,0:T(8,128)(2,1)S(1)}, bf16[416,1024]{1,0:T(8,128)(2,1)}, u32[]{:S(2)}) copy-start(bf16[416,1024]{1,0:T(8,128)(2,1)} %copy-done.3) | copy-start | bytes 2555908
  101.1 23.0 %copy-start.1 = (bf16[1024,416]{0,1:T(8,128)(2,1)S(1)}, bf16[1024,416]{0,1:T(8,128)(2,1)}, u32[]{:S(2)}) copy-start(bf16[1024,416]{0,1:T(8,128)(2,1)} %param.5) | copy-start | bytes 2555908
  138.6 21.0 %all-to-all-start.6 = ((bf16[16,16,416]{2,1,0:T(8,128)(2,1)}), bf16[16,16,416]{2,1,0:T(8,128)(2,1)S(1)}, u32[]{:S(2)}, u32[]{:S(2)}) async-start(bf16[16,16,416]{2,1,0:T(8,128)(2,1)} %shard_map.52), calls=%async_computation.6 | async-start | bytes 524288 | tf_op jit(solution)/shard_map/all_to_all | solution.py:211
  147.8 3.1 %collective-permute-start.3 = (bf16[16,256]{1,0:T(8,128)(2,1)S(1)}, bf16[16,256]{1,0:T(8,128)(2,1)S(1)}, u32[]{:S(2)}, u32[]{:S(2)}) collective-permute-start(bf16[16,256]{1,0:T(8,128)(2,1)S(1)} %get-tuple-element.16), channel_id=1, source_target_pairs={{0,1},{1,0},{2,3},{3,2},{4,5},{5,4},{6,7},{7,6},{8,9},{9,8},{10,11... | collective-permute-start | bytes 24584 | tf_op jit(solution)/shard_map/ppermute | solution.py:283

commit v7 on v5

--- a/solution.py
+++ b/solution.py
@@ -12,7 +12,6 @@
 BLOCKS = 8
 F32, BF16 = jnp.float32, jnp.bfloat16
 VMEM_BYTES = 8 * 2**20
-FIRST_VMEM_BYTES = 60 * 2**20
 
 
 def dot(a, b):
@@ -23,7 +22,7 @@
     return lax.dot_general(a, b, (((1,), (1,)), ((), ())), preferred_element_type=F32)
 
 
-def kernel_call(body, out_shape, n_in, scalars=0, far=0, scratch=(), limit=VMEM_BYTES):
+def kernel_call(body, out_shape, n_in, scalars=0, far=0, scratch=()):
     vmem = pl.BlockSpec(memory_space=pltpu.VMEM)
     specs = [pl.BlockSpec(memory_space=pltpu.SMEM)] * scalars + [pl.BlockSpec(memory_space=pl.ANY)] * far
     single = not isinstance(out_shape, (list, tuple))
@@ -33,7 +32,7 @@
         in_specs=specs + [vmem] * n_in,
         out_specs=vmem if single else [vmem] * len(out_shape),
         scratch_shapes=scratch,
-        compiler_params=pltpu.CompilerParams(vmem_limit_bytes=limit),
+        compiler_params=pltpu.CompilerParams(vmem_limit_bytes=VMEM_BYTES),
     )
 
 
@@ -61,20 +60,14 @@
 
 
 def first_products(
-    place, gathered_far, gate_far, up_far, gate_there_far, up_there_far, out, block,
-    stream, gathered, gate, up, gate_there, up_there, sems,
+    place, gate_far, up_far, gathered, gate_there, up_there, out, block, stream, gate, up, sems
 ):
-    pairs = (
-        (gathered_far, gathered),
-        (gate_there_far, gate_there),
-        (up_there_far, up_there),
-        (gate_far, gate),
-        (up_far, up),
-    )
-    fetches = [pltpu.make_async_copy(*pair, sems.at[i]) for i, pair in enumerate(pairs)]
+    fetches = [
+        pltpu.make_async_copy(gate_far, gate, sems.at[0]),
+        pltpu.make_async_copy(up_far, up, sems.at[1]),
+    ]
     for fetch in fetches:
         fetch.start()
-    fetches[0].wait()
     n_hid, cores, lines, cols = gathered.shape
     n_blocks, rows, _ = stream.shape
     half, parts = rows // n_hid, n_blocks // cores
@@ -97,13 +90,10 @@
         jnp.concatenate([stream[which * parts + k] for k in range(parts)], axis=1)
         for which in range(cores)
     )
+    gate_sum, up_sum = dot_t(y, gate_there[...]), dot_t(y, up_there[...])
+    fetches[0].wait()
+    gate_sum += dot_t(x, gate[...])
     fetches[1].wait()
-    gate_sum = dot_t(y, gate_there[...])
-    fetches[2].wait()
-    up_sum = dot_t(y, up_there[...])
-    fetches[3].wait()
-    gate_sum += dot_t(x, gate[...])
-    fetches[4].wait()
     up_sum += dot_t(x, up[...])
     store_partial(out, gate_sum, up_sum)
 
@@ -222,20 +212,21 @@
     partial_value, block = kernel_call(
         first_products,
         [partial_shape, jax.ShapeDtypeStruct((block_rows, block_cols), BF16)],
-        0,
+        3,
         scalars=1,
-        far=5,
+        far=2,
         scratch=[
             pltpu.VMEM((BLOCKS, rows, block_cols), BF16),
-            pltpu.VMEM(copies_shape.shape, BF16),
-            *(pltpu.VMEM(gate.shape, BF16) for _ in weights),
-            pltpu.SemaphoreType.DMA((5,)),
+            pltpu.VMEM(gate.shape, BF16),
+            pltpu.VMEM(up.shape, BF16),
+            pltpu.SemaphoreType.DMA((2,)),
         ],
-        limit=FIRST_VMEM_BYTES,
     )(
         jnp.stack([core, row_block, col_block]).astype(jnp.int32),
+        pltpu.with_memory_space_constraint(gate, pltpu.HBM),
+        pltpu.with_memory_space_constraint(up, pltpu.HBM),
         gathered.reshape(copies_shape.shape),
-        *weights,
+        *weights[2:],
     )
     partial_value, down_there = lax.optimization_barrier((partial_value, down_there))
     for repeat in range(STEPS):

time: 187 us -> 186 us (level)
  transfers between devices with their start and end apart: 6 -> 6, of which waited for: 3 -> 3; matrix products, arithmetic and copies ran while one was open for 0% -> 0% of each run, Pallas kernels for 3% -> 2%
where the time goes in v7:
time: 186 us; the launch traced here: 185 us
  blocking collectives  114 us (61%)
  starting transfers between devices  38 us (20%)
  waiting for transfers between devices  21.8 us (12%)
  Pallas kernels  9.38 us (5%)
    all_to_all x6, blocking collectives, exchange(): return lax.all_to_all(parts, axes, 0, 0, tiled=True)  114 us
    all_to_all x2, starting transfers between devices, exchange(): return lax.all_to_all(parts, axes, 0, 0, tiled=True)  28.6 us
    all_to_all x2, waiting for transfers between devices, exchange(): return lax.all_to_all(parts, axes, 0, 0, tiled=True)  21 us
    ppermute x2, starting transfers between devices, per_device(): weights = (gate, up, swap(gate), swap(up))  4.84 us
  transfers between devices with their start and end apart: 6, of which 3 were waited for; matrix products, arithmetic and copies ran while one was open for 0% of the time, Pallas kernels for 2%

profile of v7, /device:TPU:1, one launch (start us, length us, event | category | flops | bytes accessed | tf_op | source)
XLA Modules:
  0.0 184.6 jit_solution(5753008320199300572)
XLA Ops:
  0.0 0.0 copy-start.3
  0.0 0.7 copy-done.3
  0.7 0.0 copy-start
  0.7 0.8 shard_map.46
  1.5 19.3 %all-to-all-start = ((bf16[128,8,256]{2,1,0:T(8,128)(2,1)}), bf16[128,8,256]{2,1,0:T(8,128)(2,1)S(1)}, u32[]{:S(2)}, u32[]{:S(2)}) async-start(bf16[128,8,256]{2,1,0:T(8,128)(2,1)} %bitcast.7), calls=%async_computation | async-start | bytes 1048576 | tf_op jit(solution)/shard_map/all_to_all | solution.py:187
  20.9 2.9 %collective-permute-start = (bf16[416,1024]{1,0:T(8,128)(2,1)}, bf16[416,1024]{1,0:T(8,128)(2,1)S(1)}, u32[]{:S(2)}, u32[]{:S(2)}) collective-permute-start(bf16[416,1024]{1,0:T(8,128)(2,1)} %bitcast.12), channel_id=1, source_target_pairs={{0,1},{1,0},{2,3},{3,2},{4,5},{5,4},{6,7},{7,6},{8,9},{9,8},{10,11... | collective-permute-start | bytes 2555912 | tf_op jit(solution)/shard_map/ppermute | solution.py:204
  23.8 1.9 %collective-permute-start.1 = (bf16[416,1024]{1,0:T(8,128)(2,1)}, bf16[416,1024]{1,0:T(8,128)(2,1)S(1)}, u32[]{:S(2)}, u32[]{:S(2)}) collective-permute-start(bf16[416,1024]{1,0:T(8,128)(2,1)} %bitcast.15), channel_id=1, source_target_pairs={{0,1},{1,0},{2,3},{3,2},{4,5},{5,4},{6,7},{7,6},{8,9},{9,8},{10,11... | collective-permute-start | bytes 2555912 | tf_op jit(solution)/shard_map/ppermute | solution.py:204
  25.7 0.0 copy-done
  25.7 2.4 %collective-permute-start.2 = (bf16[416,1024]{1,0:T(8,128)(2,1)S(1)}, bf16[416,1024]{1,0:T(8,128)(2,1)}, u32[]{:S(2)}, u32[]{:S(2)}) collective-permute-start(bf16[416,1024]{1,0:T(8,128)(2,1)S(1)} %copy-done), channel_id=1, source_target_pairs={{0,1},{1,0},{2,3},{3,2},{4,5},{5,4},{6,7},{7,6},{8,9},{9,8},{10,11... | collective-permute-start | bytes 2555912 | tf_op jit(solution)/shard_map/ppermute | solution.py:205
  28.2 0.1 pad_add_fusion.1.place
  28.2 0.0 collective-permute-done.gate_there
  28.3 0.0 collective-permute-done.1.up_there
  28.3 12.2 %all-to-all-done = bf16[128,8,256]{2,1,0:T(8,128)(2,1)S(1)} async-done(((bf16[128,8,256]{2,1,0:T(8,128)(2,1)}), bf16[128,8,256]{2,1,0:T(8,128)(2,1)S(1)}, u32[]{:S(2)}, u32[]{:S(2)}) %all-to-all-start) | async-done | bytes 524320 | tf_op jit(solution)/shard_map/all_to_all | solution.py:187
  40.4 3.2 %shard_map.47 = (bf16[8,32,416]{2,1,0:T(8,128)(2,1)S(1)}, bf16[16,256]{1,0:T(8,128)(2,1)S(1)}) custom-call(s32[3]{0:T(128)S(1)} %pad_add_fusion.1.place, bf16[416,1024]{1,0:T(8,128)(2,1)} %bitcast.13, bf16[416,1024]{1,0:T(8,128)(2,1)} %bitcast.16, bf16[64,2,8,256]{3,2,1,0:T(8,128)(2,1)S(1)} %bitcast.18, ...), custom_call_target="tpu_custom_call" | custom-call | tf_op jit(solution)/shard_map/pallas_call | solution.py:212
  43.6 0.0 collective-permute-done.2.there_far
  43.6 21.5 %all_to_all.40.parts = bf16[8,32,416]{2,1,0:T(8,128)(2,1)S(1)} all-to-all(bf16[8,32,416]{2,1,0:T(8,128)(2,1)S(1)} %get-tuple-element.13), channel_id=1, replica_groups=mesh['hid'=64,'z'=8,'core'=2] {'z'}, dimensions={0} | all-to-all | bytes 425984 | tf_op jit(solution)/shard_map/all_to_all | solution.py:187
  65.2 0.1 shard_map.48
  65.2 10.4 %all_to_all.41.hidden = bf16[8,16,416]{2,1,0:T(8,128)(2,1)S(1)} all-to-all(bf16[8,16,416]{2,1,0:T(8,128)(2,1)S(1)} %shard_map.48), channel_id=1, replica_groups=mesh['hid'=64,'z'=8,'core'=2] {'z'}, dimensions={0} | all-to-all | bytes 212992 | tf_op jit(solution)/shard_map/all_to_all | solution.py:187
  75.6 1.5 shard_map.49
  77.1 0.0 copy-start.2
  77.1 23.3 %all_to_all.42.parts = bf16[64,16,256]{2,1,0:T(8,128)(2,1)S(1)} all-to-all(bf16[64,16,256]{2,1,0:T(8,128)(2,1)S(1)} %bitcast.20), channel_id=1, replica_groups=mesh['hid'=64,'z'=8,'core'=2] {'hid'}, dimensions={0} | all-to-all | bytes 1048576 | tf_op jit(solution)/shard_map/all_to_all | solution.py:187
  100.5 0.0 copy-start.1
  100.5 0.1 shard_map.50
  100.6 22.9 %all_to_all.43 = bf16[64,16,256]{2,1,0:T(8,128)(2,1)S(1)} all-to-all(bf16[64,16,256]{2,1,0:T(8,128)(2,1)S(1)} %get-tuple-element.15), channel_id=1, replica_groups=mesh['hid'=64,'z'=8,'core'=2] {'hid'}, dimensions={0} | all-to-all | bytes 1048576 | tf_op jit(solution)/shard_map/all_to_all | solution.py:187
  123.5 0.0 copy-done.2
  123.5 0.0 copy-done.1
  123.5 1.1 shard_map.51
  124.6 12.5 %all_to_all.44.parts = bf16[8,32,416]{2,1,0:T(8,128)(2,1)S(1)} all-to-all(bf16[8,32,416]{2,1,0:T(8,128)(2,1)S(1)} %shard_map.51), channel_id=1, replica_groups=mesh['hid'=64,'z'=8,'core'=2] {'z'}, dimensions={0} | all-to-all | bytes 425984 | tf_op jit(solution)/shard_map/all_to_all | solution.py:187
  137.1 0.8 shard_map.52
  137.9 9.3 %all-to-all-start.6 = ((bf16[16,16,416]{2,1,0:T(8,128)(2,1)}), bf16[16,16,416]{2,1,0:T(8,128)(2,1)S(1)}, u32[]{:S(2)}, u32[]{:S(2)}) async-start(bf16[16,16,416]{2,1,0:T(8,128)(2,1)} %shard_map.52), calls=%async_computation.6 | async-start | bytes 524288 | tf_op jit(solution)/shard_map/all_to_all | solution.py:187
  147.2 2.2 %collective-permute-start.3 = (bf16[16,256]{1,0:T(8,128)(2,1)S(1)}, bf16[16,256]{1,0:T(8,128)(2,1)S(1)}, u32[]{:S(2)}, u32[]{:S(2)}) collective-permute-start(bf16[16,256]{1,0:T(8,128)(2,1)S(1)} %get-tuple-element.16), channel_id=1, source_target_pairs={{0,1},{1,0},{2,3},{3,2},{4,5},{5,4},{6,7},{7,6},{8,9},{9,8},{10,11... | collective-permute-start | bytes 24584 | tf_op jit(solution)/shard_map/ppermute | solution.py:261
  149.3 0.1 pad_add_fusion.place
  149.4 0.8 collective-permute-done.3
  150.2 8.8 %all-to-all-done.6.hidden = bf16[16,16,416]{2,1,0:T(8,128)(2,1)S(1)} async-done(((bf16[16,16,416]{2,1,0:T(8,128)(2,1)}), bf16[16,16,416]{2,1,0:T(8,128)(2,1)S(1)}, u32[]{:S(2)}, u32[]{:S(2)}) %all-to-all-start.6) | async-done | bytes 213024 | tf_op jit(solution)/shard_map/all_to_all | solution.py:187
  159.0 1.1 shard_map.53
  160.2 23.7 %all_to_all.45.parts = bf16[64,16,256]{2,1,0:T(8,128)(2,1)S(1)} all-to-all(bf16[64,16,256]{2,1,0:T(8,128)(2,1)S(1)} %bitcast.19), channel_id=1, replica_groups=mesh['hid'=64,'z'=8,'core'=2] {'hid'}, dimensions={0} | all-to-all | bytes 1048576 | tf_op jit(solution)/shard_map/all_to_all | solution.py:187
  183.9 0.7 shard_map.54
  (1 shorter events, 0.0 us)
Async XLA Ops:
  0.0 0.7 copy-start.3
  0.7 25.0 %copy-start = (bf16[416,1024]{1,0:T(8,128)(2,1)S(1)}, bf16[416,1024]{1,0:T(8,128)(2,1)}, u32[]{:S(2)}) copy-start(bf16[416,1024]{1,0:T(8,128)(2,1)} %down.3) | copy-start | bytes 2555908
  1.5 38.9 %all-to-all-start = ((bf16[128,8,256]{2,1,0:T(8,128)(2,1)}), bf16[128,8,256]{2,1,0:T(8,128)(2,1)S(1)}, u32[]{:S(2)}, u32[]{:S(2)}) async-start(bf16[128,8,256]{2,1,0:T(8,128)(2,1)} %bitcast.7), calls=%async_computation | async-start | bytes 1048576 | tf_op jit(solution)/shard_map/all_to_all | solution.py:187
  20.9 7.4 %collective-permute-start = (bf16[416,1024]{1,0:T(8,128)(2,1)}, bf16[416,1024]{1,0:T(8,128)(2,1)S(1)}, u32[]{:S(2)}, u32[]{:S(2)}) collective-permute-start(bf16[416,1024]{1,0:T(8,128)(2,1)} %bitcast.12), channel_id=1, source_target_pairs={{0,1},{1,0},{2,3},{3,2},{4,5},{5,4},{6,7},{7,6},{8,9},{9,8},{10,11... | collective-permute-start | bytes 2555912 | tf_op jit(solution)/shard_map/ppermute | solution.py:204
  23.8 4.5 %collective-permute-start.1 = (bf16[416,1024]{1,0:T(8,128)(2,1)}, bf16[416,1024]{1,0:T(8,128)(2,1)S(1)}, u32[]{:S(2)}, u32[]{:S(2)}) collective-permute-start(bf16[416,1024]{1,0:T(8,128)(2,1)} %bitcast.15), channel_id=1, source_target_pairs={{0,1},{1,0},{2,3},{3,2},{4,5},{5,4},{6,7},{7,6},{8,9},{9,8},{10,11... | collective-permute-start | bytes 2555912 | tf_op jit(solution)/shard_map/ppermute | solution.py:204
  25.7 17.9 %collective-permute-start.2 = (bf16[416,1024]{1,0:T(8,128)(2,1)S(1)}, bf16[416,1024]{1,0:T(8,128)(2,1)}, u32[]{:S(2)}, u32[]{:S(2)}) collective-permute-start(bf16[416,1024]{1,0:T(8,128)(2,1)S(1)} %copy-done), channel_id=1, source_target_pairs={{0,1},{1,0},{2,3},{3,2},{4,5},{5,4},{6,7},{7,6},{8,9},{9,8},{10,11... | collective-permute-start | bytes 2555912 | tf_op jit(solution)/shard_map/ppermute | solution.py:205
  77.1 46.4 %copy-start.2 = (bf16[1024,416]{0,1:T(8,128)(2,1)S(1)}, bf16[1024,416]{0,1:T(8,128)(2,1)}, u32[]{:S(2)}) copy-start(bf16[1024,416]{0,1:T(8,128)(2,1)} %param.6) | copy-start | bytes 2555908
  100.5 23.0 %copy-start.1 = (bf16[1024,416]{0,1:T(8,128)(2,1)S(1)}, bf16[1024,416]{0,1:T(8,128)(2,1)}, u32[]{:S(2)}) copy-start(bf16[1024,416]{0,1:T(8,128)(2,1)} %param.5) | copy-start | bytes 2555908
  137.9 21.2 %all-to-all-start.6 = ((bf16[16,16,416]{2,1,0:T(8,128)(2,1)}), bf16[16,16,416]{2,1,0:T(8,128)(2,1)S(1)}, u32[]{:S(2)}, u32[]{:S(2)}) async-start(bf16[16,16,416]{2,1,0:T(8,128)(2,1)} %shard_map.52), calls=%async_computation.6 | async-start | bytes 524288 | tf_op jit(solution)/shard_map/all_to_all | solution.py:187
  147.2 3.1 %collective-permute-start.3 = (bf16[16,256]{1,0:T(8,128)(2,1)S(1)}, bf16[16,256]{1,0:T(8,128)(2,1)S(1)}, u32[]{:S(2)}, u32[]{:S(2)}) collective-permute-start(bf16[16,256]{1,0:T(8,128)(2,1)S(1)} %get-tuple-element.16), channel_id=1, source_target_pairs={{0,1},{1,0},{2,3},{3,2},{4,5},{5,4},{6,7},{7,6},{8,9},{9,8},{10,11... | collective-permute-start | bytes 24584 | tf_op jit(solution)/shard_map/ppermute | solution.py:261

commit v8 on v7

--- a/solution.py
+++ b/solution.py
@@ -73,7 +73,7 @@
     half, parts = rows // n_hid, n_blocks // cores
     owners = min(n_hid, 256 // lines)
     size = owners * lines
-    line = lax.broadcasted_iota(jnp.int32, (size, size), 0)
+    line = lax.broadcasted_iota(jnp.int32, (size, 1), 0)
     k, row = line // (owners * half), line % (owners * half)
     source = row // half * lines + row % half * parts + k
     order = (source == lax.broadcasted_iota(jnp.int32, (size, size), 1)).astype(F32).astype(BF16)
@@ -149,16 +149,13 @@
     n, rows, units = hidden.shape
     total, cols = n * rows, block.shape[1]
 
-    def source(width):
-        row = lax.broadcasted_iota(jnp.int32, (total, width), 0)
-        group, inner = row & ~(CORES * rows - 1), row & (CORES * rows - 1)
-        pair = CORES * (rows // BLOCKS)
-        owner, within = inner // pair, inner % pair
-        return group + within // (pair // CORES) * rows + owner * (pair // CORES) + within % (pair // CORES)
-
-    order = source(total) == lax.broadcasted_iota(jnp.int32, (total, total), 1)
+    row = lax.broadcasted_iota(jnp.int32, (total, 1), 0)
+    pair = CORES * (rows // BLOCKS)
+    inner, within, half = row % (CORES * rows), row % pair, pair // CORES
+    source = row - inner + within // half * rows + inner // pair * half + within % half
+    order = source == lax.broadcasted_iota(jnp.int32, (total, total), 1)
     x = dot(order.astype(F32).astype(BF16), hidden[...].reshape(total, units)).astype(BF16)
-    own_rows = source(rows) == lax.broadcasted_iota(jnp.int32, (total, rows), 1) + place[0] * rows
+    own_rows = source == lax.broadcasted_iota(jnp.int32, (total, rows), 1) + place[0] * rows
     addend = dot(own_rows.astype(F32).astype(BF16), block[...])
     n_blocks, own = down.shape[1] // cols, out.shape[2] // (down.shape[1] // cols)
     values, rolled = [], []

time: 186 us -> 186 us (level)
  no operation moved by 1% of the time
where the time goes in v8:
time: 186 us; the launch traced here: 185 us
  blocking collectives  114 us (61%)
  starting transfers between devices  38 us (20%)
  waiting for transfers between devices  21.8 us (12%)
  Pallas kernels  9.37 us (5%)
    all_to_all x6, blocking collectives, exchange(): return lax.all_to_all(parts, axes, 0, 0, tiled=True)  114 us
    all_to_all x2, starting transfers between devices, exchange(): return lax.all_to_all(parts, axes, 0, 0, tiled=True)  28.6 us
    all_to_all x2, waiting for transfers between devices, exchange(): return lax.all_to_all(parts, axes, 0, 0, tiled=True)  21 us
    ppermute x2, starting transfers between devices, per_device(): weights = (gate, up, swap(gate), swap(up))  4.84 us
  transfers between devices with their start and end apart: 6, of which 3 were waited for; matrix products, arithmetic and copies ran while one was open for 0% of the time, Pallas kernels for 2%

profile of v8, /device:TPU:1, one launch (start us, length us, event | category | flops | bytes accessed | tf_op | source)
XLA Modules:
  0.0 184.6 jit_solution(12656826312885037995)
XLA Ops:
  0.0 0.0 copy-start.3
  0.0 0.7 copy-done.3
  0.7 0.0 copy-start
  0.7 0.8 shard_map.46
  1.5 19.3 %all-to-all-start = ((bf16[128,8,256]{2,1,0:T(8,128)(2,1)}), bf16[128,8,256]{2,1,0:T(8,128)(2,1)S(1)}, u32[]{:S(2)}, u32[]{:S(2)}) async-start(bf16[128,8,256]{2,1,0:T(8,128)(2,1)} %bitcast.7), calls=%async_computation | async-start | bytes 1048576 | tf_op jit(solution)/shard_map/all_to_all | solution.py:184
  20.9 2.9 %collective-permute-start = (bf16[416,1024]{1,0:T(8,128)(2,1)}, bf16[416,1024]{1,0:T(8,128)(2,1)S(1)}, u32[]{:S(2)}, u32[]{:S(2)}) collective-permute-start(bf16[416,1024]{1,0:T(8,128)(2,1)} %bitcast.12), channel_id=1, source_target_pairs={{0,1},{1,0},{2,3},{3,2},{4,5},{5,4},{6,7},{7,6},{8,9},{9,8},{10,11... | collective-permute-start | bytes 2555912 | tf_op jit(solution)/shard_map/ppermute | solution.py:201
  23.8 1.9 %collective-permute-start.1 = (bf16[416,1024]{1,0:T(8,128)(2,1)}, bf16[416,1024]{1,0:T(8,128)(2,1)S(1)}, u32[]{:S(2)}, u32[]{:S(2)}) collective-permute-start(bf16[416,1024]{1,0:T(8,128)(2,1)} %bitcast.15), channel_id=1, source_target_pairs={{0,1},{1,0},{2,3},{3,2},{4,5},{5,4},{6,7},{7,6},{8,9},{9,8},{10,11... | collective-permute-start | bytes 2555912 | tf_op jit(solution)/shard_map/ppermute | solution.py:201
  25.7 0.0 copy-done
  25.7 2.4 %collective-permute-start.2 = (bf16[416,1024]{1,0:T(8,128)(2,1)S(1)}, bf16[416,1024]{1,0:T(8,128)(2,1)}, u32[]{:S(2)}, u32[]{:S(2)}) collective-permute-start(bf16[416,1024]{1,0:T(8,128)(2,1)S(1)} %copy-done), channel_id=1, source_target_pairs={{0,1},{1,0},{2,3},{3,2},{4,5},{5,4},{6,7},{7,6},{8,9},{9,8},{10,11... | collective-permute-start | bytes 2555912 | tf_op jit(solution)/shard_map/ppermute | solution.py:202
  28.2 0.1 pad_add_fusion.1.place
  28.2 0.0 collective-permute-done.gate_there
  28.3 0.0 collective-permute-done.1.up_there
  28.3 12.2 %all-to-all-done = bf16[128,8,256]{2,1,0:T(8,128)(2,1)S(1)} async-done(((bf16[128,8,256]{2,1,0:T(8,128)(2,1)}), bf16[128,8,256]{2,1,0:T(8,128)(2,1)S(1)}, u32[]{:S(2)}, u32[]{:S(2)}) %all-to-all-start) | async-done | bytes 524320 | tf_op jit(solution)/shard_map/all_to_all | solution.py:184
  40.4 3.2 %shard_map.47 = (bf16[8,32,416]{2,1,0:T(8,128)(2,1)S(1)}, bf16[16,256]{1,0:T(8,128)(2,1)S(1)}) custom-call(s32[3]{0:T(128)S(1)} %pad_add_fusion.1.place, bf16[416,1024]{1,0:T(8,128)(2,1)} %bitcast.13, bf16[416,1024]{1,0:T(8,128)(2,1)} %bitcast.16, bf16[64,2,8,256]{3,2,1,0:T(8,128)(2,1)S(1)} %bitcast.18, ...), custom_call_target="tpu_custom_call" | custom-call | tf_op jit(solution)/shard_map/pallas_call | solution.py:209
  43.6 0.0 collective-permute-done.2.there_far
  43.6 21.5 %all_to_all.40.parts = bf16[8,32,416]{2,1,0:T(8,128)(2,1)S(1)} all-to-all(bf16[8,32,416]{2,1,0:T(8,128)(2,1)S(1)} %get-tuple-element.13), channel_id=1, replica_groups=mesh['hid'=64,'z'=8,'core'=2] {'z'}, dimensions={0} | all-to-all | bytes 425984 | tf_op jit(solution)/shard_map/all_to_all | solution.py:184
  65.2 0.1 shard_map.48
  65.2 10.4 %all_to_all.41.hidden = bf16[8,16,416]{2,1,0:T(8,128)(2,1)S(1)} all-to-all(bf16[8,16,416]{2,1,0:T(8,128)(2,1)S(1)} %shard_map.48), channel_id=1, replica_groups=mesh['hid'=64,'z'=8,'core'=2] {'z'}, dimensions={0} | all-to-all | bytes 212992 | tf_op jit(solution)/shard_map/all_to_all | solution.py:184
  75.6 1.5 shard_map.49
  77.1 0.0 copy-start.2
  77.1 23.3 %all_to_all.42.parts = bf16[64,16,256]{2,1,0:T(8,128)(2,1)S(1)} all-to-all(bf16[64,16,256]{2,1,0:T(8,128)(2,1)S(1)} %bitcast.20), channel_id=1, replica_groups=mesh['hid'=64,'z'=8,'core'=2] {'hid'}, dimensions={0} | all-to-all | bytes 1048576 | tf_op jit(solution)/shard_map/all_to_all | solution.py:184
  100.5 0.0 copy-start.1
  100.5 0.1 shard_map.50
  100.6 22.9 %all_to_all.43 = bf16[64,16,256]{2,1,0:T(8,128)(2,1)S(1)} all-to-all(bf16[64,16,256]{2,1,0:T(8,128)(2,1)S(1)} %get-tuple-element.15), channel_id=1, replica_groups=mesh['hid'=64,'z'=8,'core'=2] {'hid'}, dimensions={0} | all-to-all | bytes 1048576 | tf_op jit(solution)/shard_map/all_to_all | solution.py:184
  123.5 0.0 copy-done.2
  123.5 0.0 copy-done.1
  123.5 1.1 shard_map.51
  124.6 12.5 %all_to_all.44.parts = bf16[8,32,416]{2,1,0:T(8,128)(2,1)S(1)} all-to-all(bf16[8,32,416]{2,1,0:T(8,128)(2,1)S(1)} %shard_map.51), channel_id=1, replica_groups=mesh['hid'=64,'z'=8,'core'=2] {'z'}, dimensions={0} | all-to-all | bytes 425984 | tf_op jit(solution)/shard_map/all_to_all | solution.py:184
  137.1 0.8 shard_map.52
  137.9 9.3 %all-to-all-start.6 = ((bf16[16,16,416]{2,1,0:T(8,128)(2,1)}), bf16[16,16,416]{2,1,0:T(8,128)(2,1)S(1)}, u32[]{:S(2)}, u32[]{:S(2)}) async-start(bf16[16,16,416]{2,1,0:T(8,128)(2,1)} %shard_map.52), calls=%async_computation.6 | async-start | bytes 524288 | tf_op jit(solution)/shard_map/all_to_all | solution.py:184
  147.2 2.2 %collective-permute-start.3 = (bf16[16,256]{1,0:T(8,128)(2,1)S(1)}, bf16[16,256]{1,0:T(8,128)(2,1)S(1)}, u32[]{:S(2)}, u32[]{:S(2)}) collective-permute-start(bf16[16,256]{1,0:T(8,128)(2,1)S(1)} %get-tuple-element.16), channel_id=1, source_target_pairs={{0,1},{1,0},{2,3},{3,2},{4,5},{5,4},{6,7},{7,6},{8,9},{9,8},{10,11... | collective-permute-start | bytes 24584 | tf_op jit(solution)/shard_map/ppermute | solution.py:258
  149.3 0.1 pad_add_fusion.place
  149.4 0.8 collective-permute-done.3
  150.2 8.8 %all-to-all-done.6.hidden = bf16[16,16,416]{2,1,0:T(8,128)(2,1)S(1)} async-done(((bf16[16,16,416]{2,1,0:T(8,128)(2,1)}), bf16[16,16,416]{2,1,0:T(8,128)(2,1)S(1)}, u32[]{:S(2)}, u32[]{:S(2)}) %all-to-all-start.6) | async-done | bytes 213024 | tf_op jit(solution)/shard_map/all_to_all | solution.py:184
  159.0 1.1 shard_map.53
  160.2 23.7 %all_to_all.45.parts = bf16[64,16,256]{2,1,0:T(8,128)(2,1)S(1)} all-to-all(bf16[64,16,256]{2,1,0:T(8,128)(2,1)S(1)} %bitcast.19), channel_id=1, replica_groups=mesh['hid'=64,'z'=8,'core'=2] {'hid'}, dimensions={0} | all-to-all | bytes 1048576 | tf_op jit(solution)/shard_map/all_to_all | solution.py:184
  183.9 0.7 shard_map.54
  (1 shorter events, 0.0 us)
Async XLA Ops:
  0.0 0.7 copy-start.3
  0.7 25.0 %copy-start = (bf16[416,1024]{1,0:T(8,128)(2,1)S(1)}, bf16[416,1024]{1,0:T(8,128)(2,1)}, u32[]{:S(2)}) copy-start(bf16[416,1024]{1,0:T(8,128)(2,1)} %down.3) | copy-start | bytes 2555908
  1.5 38.9 %all-to-all-start = ((bf16[128,8,256]{2,1,0:T(8,128)(2,1)}), bf16[128,8,256]{2,1,0:T(8,128)(2,1)S(1)}, u32[]{:S(2)}, u32[]{:S(2)}) async-start(bf16[128,8,256]{2,1,0:T(8,128)(2,1)} %bitcast.7), calls=%async_computation | async-start | bytes 1048576 | tf_op jit(solution)/shard_map/all_to_all | solution.py:184
  20.9 7.4 %collective-permute-start = (bf16[416,1024]{1,0:T(8,128)(2,1)}, bf16[416,1024]{1,0:T(8,128)(2,1)S(1)}, u32[]{:S(2)}, u32[]{:S(2)}) collective-permute-start(bf16[416,1024]{1,0:T(8,128)(2,1)} %bitcast.12), channel_id=1, source_target_pairs={{0,1},{1,0},{2,3},{3,2},{4,5},{5,4},{6,7},{7,6},{8,9},{9,8},{10,11... | collective-permute-start | bytes 2555912 | tf_op jit(solution)/shard_map/ppermute | solution.py:201
  23.8 4.5 %collective-permute-start.1 = (bf16[416,1024]{1,0:T(8,128)(2,1)}, bf16[416,1024]{1,0:T(8,128)(2,1)S(1)}, u32[]{:S(2)}, u32[]{:S(2)}) collective-permute-start(bf16[416,1024]{1,0:T(8,128)(2,1)} %bitcast.15), channel_id=1, source_target_pairs={{0,1},{1,0},{2,3},{3,2},{4,5},{5,4},{6,7},{7,6},{8,9},{9,8},{10,11... | collective-permute-start | bytes 2555912 | tf_op jit(solution)/shard_map/ppermute | solution.py:201
  25.7 17.9 %collective-permute-start.2 = (bf16[416,1024]{1,0:T(8,128)(2,1)S(1)}, bf16[416,1024]{1,0:T(8,128)(2,1)}, u32[]{:S(2)}, u32[]{:S(2)}) collective-permute-start(bf16[416,1024]{1,0:T(8,128)(2,1)S(1)} %copy-done), channel_id=1, source_target_pairs={{0,1},{1,0},{2,3},{3,2},{4,5},{5,4},{6,7},{7,6},{8,9},{9,8},{10,11... | collective-permute-start | bytes 2555912 | tf_op jit(solution)/shard_map/ppermute | solution.py:202
  77.1 46.4 %copy-start.2 = (bf16[1024,416]{0,1:T(8,128)(2,1)S(1)}, bf16[1024,416]{0,1:T(8,128)(2,1)}, u32[]{:S(2)}) copy-start(bf16[1024,416]{0,1:T(8,128)(2,1)} %param.6) | copy-start | bytes 2555908
  100.5 23.0 %copy-start.1 = (bf16[1024,416]{0,1:T(8,128)(2,1)S(1)}, bf16[1024,416]{0,1:T(8,128)(2,1)}, u32[]{:S(2)}) copy-start(bf16[1024,416]{0,1:T(8,128)(2,1)} %param.5) | copy-start | bytes 2555908
  137.9 21.2 %all-to-all-start.6 = ((bf16[16,16,416]{2,1,0:T(8,128)(2,1)}), bf16[16,16,416]{2,1,0:T(8,128)(2,1)S(1)}, u32[]{:S(2)}, u32[]{:S(2)}) async-start(bf16[16,16,416]{2,1,0:T(8,128)(2,1)} %shard_map.52), calls=%async_computation.6 | async-start | bytes 524288 | tf_op jit(solution)/shard_map/all_to_all | solution.py:184
  147.2 3.1 %collective-permute-start.3 = (bf16[16,256]{1,0:T(8,128)(2,1)S(1)}, bf16[16,256]{1,0:T(8,128)(2,1)S(1)}, u32[]{:S(2)}, u32[]{:S(2)}) collective-permute-start(bf16[16,256]{1,0:T(8,128)(2,1)S(1)} %get-tuple-element.16), channel_id=1, source_target_pairs={{0,1},{1,0},{2,3},{3,2},{4,5},{5,4},{6,7},{7,6},{8,9},{9,8},{10,11... | collective-permute-start | bytes 24584 | tf_op jit(solution)/shard_map/ppermute | solution.py:258

commit v9 on v8

--- a/solution.py
+++ b/solution.py
@@ -37,9 +37,10 @@
 
 
 def store_partial(out, gate, up):
-    n, two, units = out.shape
-    out[:, : two // 2, :] = gate.astype(BF16).reshape(n, two // 2, units)
-    out[:, two // 2 :, :] = up.astype(BF16).reshape(n, two // 2, units)
+    n, rows, width = out.shape
+    units = width // 2
+    out[:, :, :units] = gate.astype(BF16).reshape(n, rows, units)
+    out[:, :, units:] = up.astype(BF16).reshape(n, rows, units)
 
 
 def copy_tokens(tokens, out):
@@ -115,8 +116,8 @@
     total = parts[0].astype(F32)
     for k in range(1, parts.shape[0]):
         total += parts[k].astype(F32)
-    rows = total.shape[0] // 2
-    gate, up = total[:rows], total[rows:]
+    units = total.shape[1] // 2
+    gate, up = total[:, :units], total[:, units:]
     hidden = (gate / (1.0 + jnp.exp(-gate)) * up).astype(BF16)
     for k in range(out.shape[0]):
         out[k] = hidden
@@ -205,7 +206,7 @@
     copies_shape = jax.ShapeDtypeStruct((n_hid, CORES, lines, block_cols), BF16)
     copies = kernel_call(copy_tokens, copies_shape, 1)(tokens)
     gathered = exchange(copies.reshape(n_hid * CORES, lines, block_cols), ("hid", "core"))
-    partial_shape = jax.ShapeDtypeStruct((n_z, 2 * chunk, units), BF16)
+    partial_shape = jax.ShapeDtypeStruct((n_z, chunk, 2 * units), BF16)
     partial_value, block = kernel_call(
         first_products,
         [partial_shape, jax.ShapeDtypeStruct((block_rows, block_cols), BF16)],

time: 186 us -> 185 us (level)
  no operation moved by 1% of the time
where the time goes in v9:
time: 185 us; the launch traced here: 184 us
  blocking collectives  113 us (61%)
  starting transfers between devices  37.7 us (20%)
  waiting for transfers between devices  21.8 us (12%)
  Pallas kernels  9.6 us (5%)
    all_to_all x6, blocking collectives, exchange(): return lax.all_to_all(parts, axes, 0, 0, tiled=True)  113 us
    all_to_all x2, starting transfers between devices, exchange(): return lax.all_to_all(parts, axes, 0, 0, tiled=True)  28.3 us
    all_to_all x2, waiting for transfers between devices, exchange(): return lax.all_to_all(parts, axes, 0, 0, tiled=True)  21 us
    ppermute x2, starting transfers between devices, per_device(): weights = (gate, up, swap(gate), swap(up))  4.84 us
  transfers between devices with their start and end apart: 6, of which 3 were waited for; matrix products, arithmetic and copies ran while one was open for 0% of the time, Pallas kernels for 2%

profile of v9, /device:TPU:1, one launch (start us, length us, event | category | flops | bytes accessed | tf_op | source)
XLA Modules:
  0.0 183.6 jit_solution(3751242473772008198)
XLA Ops:
  0.0 0.0 copy-start.3
  0.0 0.7 copy-done.3
  0.7 0.0 copy-start
  0.7 0.8 shard_map.46
  1.5 19.3 %all-to-all-start = ((bf16[128,8,256]{2,1,0:T(8,128)(2,1)}), bf16[128,8,256]{2,1,0:T(8,128)(2,1)S(1)}, u32[]{:S(2)}, u32[]{:S(2)}) async-start(bf16[128,8,256]{2,1,0:T(8,128)(2,1)} %bitcast.7), calls=%async_computation | async-start | bytes 1048576 | tf_op jit(solution)/shard_map/all_to_all | solution.py:185
  20.9 2.9 %collective-permute-start = (bf16[416,1024]{1,0:T(8,128)(2,1)}, bf16[416,1024]{1,0:T(8,128)(2,1)S(1)}, u32[]{:S(2)}, u32[]{:S(2)}) collective-permute-start(bf16[416,1024]{1,0:T(8,128)(2,1)} %bitcast.12), channel_id=1, source_target_pairs={{0,1},{1,0},{2,3},{3,2},{4,5},{5,4},{6,7},{7,6},{8,9},{9,8},{10,11... | collective-permute-start | bytes 2555912 | tf_op jit(solution)/shard_map/ppermute | solution.py:202
  23.8 1.9 %collective-permute-start.1 = (bf16[416,1024]{1,0:T(8,128)(2,1)}, bf16[416,1024]{1,0:T(8,128)(2,1)S(1)}, u32[]{:S(2)}, u32[]{:S(2)}) collective-permute-start(bf16[416,1024]{1,0:T(8,128)(2,1)} %bitcast.15), channel_id=1, source_target_pairs={{0,1},{1,0},{2,3},{3,2},{4,5},{5,4},{6,7},{7,6},{8,9},{9,8},{10,11... | collective-permute-start | bytes 2555912 | tf_op jit(solution)/shard_map/ppermute | solution.py:202
  25.7 0.0 copy-done
  25.7 2.4 %collective-permute-start.2 = (bf16[416,1024]{1,0:T(8,128)(2,1)S(1)}, bf16[416,1024]{1,0:T(8,128)(2,1)}, u32[]{:S(2)}, u32[]{:S(2)}) collective-permute-start(bf16[416,1024]{1,0:T(8,128)(2,1)S(1)} %copy-done), channel_id=1, source_target_pairs={{0,1},{1,0},{2,3},{3,2},{4,5},{5,4},{6,7},{7,6},{8,9},{9,8},{10,11... | collective-permute-start | bytes 2555912 | tf_op jit(solution)/shard_map/ppermute | solution.py:203
  28.2 0.1 pad_add_fusion.1.place
  28.2 0.0 collective-permute-done.gate_there
  28.3 0.0 collective-permute-done.1.up_there
  28.3 12.2 %all-to-all-done = bf16[128,8,256]{2,1,0:T(8,128)(2,1)S(1)} async-done(((bf16[128,8,256]{2,1,0:T(8,128)(2,1)}), bf16[128,8,256]{2,1,0:T(8,128)(2,1)S(1)}, u32[]{:S(2)}, u32[]{:S(2)}) %all-to-all-start) | async-done | bytes 524320 | tf_op jit(solution)/shard_map/all_to_all | solution.py:185
  40.4 3.2 %shard_map.47 = (bf16[8,16,832]{2,1,0:T(8,128)(2,1)S(1)}, bf16[16,256]{1,0:T(8,128)(2,1)S(1)}) custom-call(s32[3]{0:T(128)S(1)} %pad_add_fusion.1.place, bf16[416,1024]{1,0:T(8,128)(2,1)} %bitcast.13, bf16[416,1024]{1,0:T(8,128)(2,1)} %bitcast.16, bf16[64,2,8,256]{3,2,1,0:T(8,128)(2,1)S(1)} %bitcast.18, ...), custom_call_target="tpu_custom_call" | custom-call | tf_op jit(solution)/shard_map/pallas_call | solution.py:210
  43.7 0.0 collective-permute-done.2.there_far
  43.7 21.1 %all_to_all.40.parts = bf16[8,16,832]{2,1,0:T(8,128)(2,1)S(1)} all-to-all(bf16[8,16,832]{2,1,0:T(8,128)(2,1)S(1)} %get-tuple-element.13), channel_id=1, replica_groups=mesh['hid'=64,'z'=8,'core'=2] {'z'}, dimensions={0} | all-to-all | bytes 425984 | tf_op jit(solution)/shard_map/all_to_all | solution.py:185
  64.8 0.1 shard_map.48
  64.9 10.4 %all_to_all.41.hidden = bf16[8,16,416]{2,1,0:T(8,128)(2,1)S(1)} all-to-all(bf16[8,16,416]{2,1,0:T(8,128)(2,1)S(1)} %shard_map.48), channel_id=1, replica_groups=mesh['hid'=64,'z'=8,'core'=2] {'z'}, dimensions={0} | all-to-all | bytes 212992 | tf_op jit(solution)/shard_map/all_to_all | solution.py:185
  75.4 1.5 shard_map.49
  76.8 0.0 copy-start.2
  76.9 23.1 %all_to_all.42.parts = bf16[64,16,256]{2,1,0:T(8,128)(2,1)S(1)} all-to-all(bf16[64,16,256]{2,1,0:T(8,128)(2,1)S(1)} %bitcast.20), channel_id=1, replica_groups=mesh['hid'=64,'z'=8,'core'=2] {'hid'}, dimensions={0} | all-to-all | bytes 1048576 | tf_op jit(solution)/shard_map/all_to_all | solution.py:185
  99.9 0.0 copy-start.1
  99.9 0.1 shard_map.50
  100.1 24.0 %all_to_all.43 = bf16[64,16,256]{2,1,0:T(8,128)(2,1)S(1)} all-to-all(bf16[64,16,256]{2,1,0:T(8,128)(2,1)S(1)} %get-tuple-element.15), channel_id=1, replica_groups=mesh['hid'=64,'z'=8,'core'=2] {'hid'}, dimensions={0} | all-to-all | bytes 1048576 | tf_op jit(solution)/shard_map/all_to_all | solution.py:185
  124.0 0.0 copy-done.2
  124.0 0.0 copy-done.1
  124.0 1.2 shard_map.51
  125.2 11.4 %all_to_all.44.parts = bf16[8,16,832]{2,1,0:T(8,128)(2,1)S(1)} all-to-all(bf16[8,16,832]{2,1,0:T(8,128)(2,1)S(1)} %shard_map.51), channel_id=1, replica_groups=mesh['hid'=64,'z'=8,'core'=2] {'z'}, dimensions={0} | all-to-all | bytes 425984 | tf_op jit(solution)/shard_map/all_to_all | solution.py:185
  136.6 0.8 shard_map.52
  137.4 9.0 %all-to-all-start.6 = ((bf16[16,16,416]{2,1,0:T(8,128)(2,1)}), bf16[16,16,416]{2,1,0:T(8,128)(2,1)S(1)}, u32[]{:S(2)}, u32[]{:S(2)}) async-start(bf16[16,16,416]{2,1,0:T(8,128)(2,1)} %shard_map.52), calls=%async_computation.6 | async-start | bytes 524288 | tf_op jit(solution)/shard_map/all_to_all | solution.py:185
  146.4 2.2 %collective-permute-start.3 = (bf16[16,256]{1,0:T(8,128)(2,1)S(1)}, bf16[16,256]{1,0:T(8,128)(2,1)S(1)}, u32[]{:S(2)}, u32[]{:S(2)}) collective-permute-start(bf16[16,256]{1,0:T(8,128)(2,1)S(1)} %get-tuple-element.16), channel_id=1, source_target_pairs={{0,1},{1,0},{2,3},{3,2},{4,5},{5,4},{6,7},{7,6},{8,9},{9,8},{10,11... | collective-permute-start | bytes 24584 | tf_op jit(solution)/shard_map/ppermute | solution.py:259
  148.6 0.1 pad_add_fusion.place
  148.7 0.8 collective-permute-done.3
  149.5 8.8 %all-to-all-done.6.hidden = bf16[16,16,416]{2,1,0:T(8,128)(2,1)S(1)} async-done(((bf16[16,16,416]{2,1,0:T(8,128)(2,1)}), bf16[16,16,416]{2,1,0:T(8,128)(2,1)S(1)}, u32[]{:S(2)}, u32[]{:S(2)}) %all-to-all-start.6) | async-done | bytes 213024 | tf_op jit(solution)/shard_map/all_to_all | solution.py:185
  158.3 1.1 shard_map.53
  159.4 23.4 %all_to_all.45.parts = bf16[64,16,256]{2,1,0:T(8,128)(2,1)S(1)} all-to-all(bf16[64,16,256]{2,1,0:T(8,128)(2,1)S(1)} %bitcast.19), channel_id=1, replica_groups=mesh['hid'=64,'z'=8,'core'=2] {'hid'}, dimensions={0} | all-to-all | bytes 1048576 | tf_op jit(solution)/shard_map/all_to_all | solution.py:185
  182.9 0.7 shard_map.54
  (1 shorter events, 0.0 us)
Async XLA Ops:
  0.0 0.7 copy-start.3
  0.7 25.0 %copy-start = (bf16[416,1024]{1,0:T(8,128)(2,1)S(1)}, bf16[416,1024]{1,0:T(8,128)(2,1)}, u32[]{:S(2)}) copy-start(bf16[416,1024]{1,0:T(8,128)(2,1)} %down.3) | copy-start | bytes 2555908
  1.5 38.9 %all-to-all-start = ((bf16[128,8,256]{2,1,0:T(8,128)(2,1)}), bf16[128,8,256]{2,1,0:T(8,128)(2,1)S(1)}, u32[]{:S(2)}, u32[]{:S(2)}) async-start(bf16[128,8,256]{2,1,0:T(8,128)(2,1)} %bitcast.7), calls=%async_computation | async-start | bytes 1048576 | tf_op jit(solution)/shard_map/all_to_all | solution.py:185
  20.9 7.4 %collective-permute-start = (bf16[416,1024]{1,0:T(8,128)(2,1)}, bf16[416,1024]{1,0:T(8,128)(2,1)S(1)}, u32[]{:S(2)}, u32[]{:S(2)}) collective-permute-start(bf16[416,1024]{1,0:T(8,128)(2,1)} %bitcast.12), channel_id=1, source_target_pairs={{0,1},{1,0},{2,3},{3,2},{4,5},{5,4},{6,7},{7,6},{8,9},{9,8},{10,11... | collective-permute-start | bytes 2555912 | tf_op jit(solution)/shard_map/ppermute | solution.py:202
  23.8 4.5 %collective-permute-start.1 = (bf16[416,1024]{1,0:T(8,128)(2,1)}, bf16[416,1024]{1,0:T(8,128)(2,1)S(1)}, u32[]{:S(2)}, u32[]{:S(2)}) collective-permute-start(bf16[416,1024]{1,0:T(8,128)(2,1)} %bitcast.15), channel_id=1, source_target_pairs={{0,1},{1,0},{2,3},{3,2},{4,5},{5,4},{6,7},{7,6},{8,9},{9,8},{10,11... | collective-permute-start | bytes 2555912 | tf_op jit(solution)/shard_map/ppermute | solution.py:202
  25.7 18.0 %collective-permute-start.2 = (bf16[416,1024]{1,0:T(8,128)(2,1)S(1)}, bf16[416,1024]{1,0:T(8,128)(2,1)}, u32[]{:S(2)}, u32[]{:S(2)}) collective-permute-start(bf16[416,1024]{1,0:T(8,128)(2,1)S(1)} %copy-done), channel_id=1, source_target_pairs={{0,1},{1,0},{2,3},{3,2},{4,5},{5,4},{6,7},{7,6},{8,9},{9,8},{10,11... | collective-permute-start | bytes 2555912 | tf_op jit(solution)/shard_map/ppermute | solution.py:203
  76.8 47.2 %copy-start.2 = (bf16[1024,416]{0,1:T(8,128)(2,1)S(1)}, bf16[1024,416]{0,1:T(8,128)(2,1)}, u32[]{:S(2)}) copy-start(bf16[1024,416]{0,1:T(8,128)(2,1)} %param.6) | copy-start | bytes 2555908
  99.9 24.1 %copy-start.1 = (bf16[1024,416]{0,1:T(8,128)(2,1)S(1)}, bf16[1024,416]{0,1:T(8,128)(2,1)}, u32[]{:S(2)}) copy-start(bf16[1024,416]{0,1:T(8,128)(2,1)} %param.5) | copy-start | bytes 2555908
  137.4 20.9 %all-to-all-start.6 = ((bf16[16,16,416]{2,1,0:T(8,128)(2,1)}), bf16[16,16,416]{2,1,0:T(8,128)(2,1)S(1)}, u32[]{:S(2)}, u32[]{:S(2)}) async-start(bf16[16,16,416]{2,1,0:T(8,128)(2,1)} %shard_map.52), calls=%async_computation.6 | async-start | bytes 524288 | tf_op jit(solution)/shard_map/all_to_all | solution.py:185
  146.4 3.1 %collective-permute-start.3 = (bf16[16,256]{1,0:T(8,128)(2,1)S(1)}, bf16[16,256]{1,0:T(8,128)(2,1)S(1)}, u32[]{:S(2)}, u32[]{:S(2)}) collective-permute-start(bf16[16,256]{1,0:T(8,128)(2,1)S(1)} %get-tuple-element.16), channel_id=1, source_target_pairs={{0,1},{1,0},{2,3},{3,2},{4,5},{5,4},{6,7},{7,6},{8,9},{9,8},{10,11... | collective-permute-start | bytes 24584 | tf_op jit(solution)/shard_map/ppermute | solution.py:259
